TPU v7x, 256 devices: a whole 4x4x8 slice. The times are simulated.
256 devices in a mesh: phase: 4 (over y), elem: 64 (over x, z, core).
Axes of the slice: x: 4, y: 4, z: 8, core: 2. Of those that a mesh axis runs over, the one named last changes fastest.
Arguments:
- state: bfloat16 [131072, 320], P(('phase', 'elem')), parts along dimension 0, may hold values from -6 to 6
- adjoint: bfloat16 [131072, 320], P(('phase', 'elem')), parts along dimension 0, may hold values from -6 to 6
- right_side: bfloat16 [131072, 320], P(('phase', 'elem')), parts along dimension 0, may hold values from -6 to 6
- source: bfloat16 [131072, 320], P(('phase', 'elem')), parts along dimension 0, may hold values from -6 to 6
- metric: float32 [8, 32768], P(None, 'elem'), may hold values from 0.5 to 2
- basis_tiles: bfloat16 [32, 320, 320], P('phase'), parts along dimension 0, may hold values from -0.125 to 0.125
- face_tiles: bfloat16 [24, 320, 320], P('phase'), parts along dimension 0, may hold values from -0.125 to 0.125
- precond: bfloat16 [1280, 320], P('phase'), parts along dimension 0, may hold values from -0.3125 to 0.3125
- wall_tile: bfloat16 [512, 320], P('phase'), parts along dimension 0, may hold values from -0.5 to 0.5
- traction_tile: bfloat16 [1280, 128], P('phase'), parts along dimension 0, may hold values from -0.3125 to 0.3125
- mode_rows: bfloat16 [65536, 128], P(('phase', 'elem')), parts along dimension 0, may hold values from -6 to 6
- neighbors: int32 [32768, 6], P('elem'), may hold values from -1 to 32767, as said below
- wall_node: int32 [32768], P('elem'), may hold values from -1 to 16383, as said below
- wall_target: int32 [16384], P('elem'), may hold values from 0 to 32767, as said below
Outputs:
- new_state: bfloat16 [131072, 320], P(('phase', 'elem')), parts along dimension 0
- new_adjoint: bfloat16 [131072, 320], P(('phase', 'elem')), parts along dimension 0
- wall_load: bfloat16 [65536, 128], P(('phase', 'elem')), parts along dimension 0
There are 4 independent parts, one for each index of `phase`. A program takes and returns all parts, laid end to end along the dimension named above; an argument that names none is the same for every part. Nothing has to cross between parts.
Inputs may be any that keep to these rules, and one draw needn't show every extreme that they name: `neighbors`: entry (e, f) is -1 where the face lies on the slab boundary, else an element at most 64 positions from e in the numbering; faces 4 and 5 lie exactly 64 positions away where they exist. `wall_target`: distinct nodes name distinct elements. Of the 256 nodes of one device at most 8 name elements of any one device, and some pair of devices reaches 8. wall_node is the inverse of wall_target: wall_node[wall_target[n]] = n, and -1 on every element that no node names.
All inputs are finite; a program needn't handle non-finite values.
Results may differ from a plain program's by a relative error of at most 0.006.
Values may be sent and summed in bfloat16 or wider, within the bound.
No kernel may reach another device: no remote copies, remote signals or barrier semaphores. Data moves between devices by JAX's collectives and lax.ppermute only.
A program may use at most 64 MiB of HBM per device.

v0:
```python
import jax
import jax.numpy as jnp
from jax import lax
from jax.sharding import PartitionSpec as P

HALO = 64


def extended_2(value, sides, width):
    for axis, dim in sides:
        devices, length = (lax.axis_size(axis), value.shape[dim])
        up = [(i, (i + 1) % devices) for i in range(devices - 1)]
        down = [(j, i) for i, j in up]
        last = lax.slice_in_dim(value, length - width, length, axis=dim)
        initial = lax.slice_in_dim(value, 0, width, axis=dim)
        before = lax.ppermute(last, axis, up)
        after = lax.ppermute(initial, axis, down)
        value = jnp.concatenate([before, value, after], axis=dim)
    return value


def shifted(block, axis, distance):
    devices = range(lax.axis_size(axis))
    route = [(i - distance, i) for i in devices if i - distance in devices]
    return lax.ppermute(block, axis, route)


def times_transposed(left, right):
    return lax.dot_general(
        left, right, (((1,), (1,)), ((), ())), preferred_element_type=jnp.float32
    )


def on_device(
    state,
    adjoint,
    right_side,
    source,
    metric,
    basis_tiles,
    face_tiles,
    precond,
    wall_tile,
    traction_tile,
    mode_rows,
    neighbors,
    wall_node,
    wall_target,
):
    elem_rows = state.shape[0]
    width = state.shape[1]
    base_row = lax.axis_index("elem") * elem_rows
    linked = neighbors >= 0
    local_index = jnp.clip(neighbors - base_row + HALO, 0, elem_rows + 2 * HALO - 1)
    geo_count = basis_tiles.shape[0]
    face_count = face_tiles.shape[0]
    on_wall = wall_node >= 0
    extended = extended_2(state, (("elem", 0),), HALO)
    applied = jnp.zeros((elem_rows, width), jnp.float32)
    for level in range(geo_count):
        product = jnp.dot(state, basis_tiles[level], preferred_element_type=jnp.float32)
        applied = applied + metric[level][:, None] * product
    for face in range(face_count):
        rows_in = jnp.where(
            linked[:, face][:, None], extended[local_index[:, face]], jnp.zeros((), jnp.bfloat16)
        )
        applied = applied + jnp.dot(rows_in, face_tiles[face], preferred_element_type=jnp.float32)
    gathered = lax.all_gather(mode_rows, "elem", axis=0, tiled=True)
    picked = gathered[jnp.maximum(wall_node, 0)]
    wall_modes = jnp.where(on_wall[:, None], picked, jnp.zeros((), jnp.bfloat16))
    forcing = jnp.dot(wall_modes, wall_tile, preferred_element_type=jnp.float32)
    residual = (right_side.astype(jnp.float32) + forcing - applied).astype(jnp.bfloat16)
    update = jnp.dot(residual, precond, preferred_element_type=jnp.float32)
    new_state = (state.astype(jnp.float32) + update / metric[0][:, None]).astype(jnp.bfloat16)
    applied_t = jnp.zeros((elem_rows, width), jnp.float32)
    for level in range(geo_count):
        applied_t = applied_t + metric[level][:, None] * times_transposed(
            adjoint, basis_tiles[level]
        )
    collected = jnp.zeros((elem_rows + 2 * HALO, width), jnp.float32)
    for face in range(face_count):
        pushed = times_transposed(adjoint, face_tiles[face]) * linked[:, face][:, None].astype(
            jnp.float32
        )
        collected = collected.at[local_index[:, face]].add(pushed)
    from_above = shifted(collected[:HALO].astype(jnp.bfloat16), "elem", -1).astype(jnp.float32)
    from_below = shifted(collected[elem_rows + HALO :].astype(jnp.bfloat16), "elem", 1).astype(
        jnp.float32
    )
    own_rows = collected[HALO : elem_rows + HALO]
    own_rows = own_rows.at[:HALO].add(from_below)
    own_rows = own_rows.at[elem_rows - HALO :].add(from_above)
    applied_t = applied_t + own_rows
    adjoint_residual = (source.astype(jnp.float32) - applied_t).astype(jnp.bfloat16)
    update_t = times_transposed(adjoint_residual, precond)
    new_adjoint = (adjoint.astype(jnp.float32) + update_t / metric[0][:, None]).astype(jnp.bfloat16)
    traction = jnp.dot(new_adjoint, traction_tile, preferred_element_type=jnp.float32).astype(
        jnp.bfloat16
    )
    gathered_load = lax.all_gather(traction, "elem", axis=0, tiled=True)
    wall_load = gathered_load[wall_target]
    return (new_state, new_adjoint, wall_load)


def solution(mesh):
    return jax.shard_map(
        on_device,
        mesh=mesh,
        in_specs=(
            P(("phase", "elem"), None),
            P(("phase", "elem"), None),
            P(("phase", "elem"), None),
            P(("phase", "elem"), None),
            P(None, "elem"),
            P("phase", None, None),
            P("phase", None, None),
            P("phase", None),
            P("phase", None),
            P("phase", None),
            P(("phase", "elem"), None),
            P("elem", None),
            P("elem"),
            P("elem"),
        ),
        out_specs=(
            P(("phase", "elem"), None),
            P(("phase", "elem"), None),
            P(("phase", "elem"), None),
        ),
        check_vma=False,
    )
```

profile of v0, /device:TPU:1, one launch (start us, length us, event | category | flops | bytes accessed | tf_op | source)
XLA Modules:
  0.0 190.2 jit_solution(16922372023001671910)
XLA Ops:
  7.2 0.7 all-gather.3.cloned.1.call-update
  8.0 0.7 broadcast_compare_fusion
  8.8 1.4 convolution_multiply_fusion.5
  10.3 1.2 copy.23
  11.5 1.2 convolution_multiply_fusion.4
  12.7 1.3 copy.24
  14.0 1.2 convolution_multiply_fusion.3
  15.2 2.3 %copy.25 = f32[512,320]{1,0:T(8,128)} copy(f32[512,320]{0,1:T(8,128)} %convolution_multiply_fusion.3) | data formatting | bytes 1310720 | tf_op jit(solution)/shard_map/mul | solution.py:82
  17.5 1.2 convolution_multiply_fusion.2
  18.7 2.2 %copy.26 = f32[512,320]{1,0:T(8,128)} copy(f32[512,320]{0,1:T(8,128)} %convolution_multiply_fusion.2) | data formatting | bytes 1310720 | tf_op jit(solution)/shard_map/mul | solution.py:82
  20.9 1.2 convolution_multiply_fusion.1
  22.1 2.3 %copy.27 = f32[512,320]{1,0:T(8,128)} copy(f32[512,320]{0,1:T(8,128)} %convolution_multiply_fusion.1) | data formatting | bytes 1310720 | tf_op jit(solution)/shard_map/mul | solution.py:82
  24.4 1.2 convolution_multiply_fusion
  25.6 2.3 %copy.28 = f32[512,320]{1,0:T(8,128)} copy(f32[512,320]{0,1:T(8,128)} %convolution_multiply_fusion) | data formatting | bytes 1310720 | tf_op jit(solution)/shard_map/mul | solution.py:82
  27.9 4.4 %scatter_custom_fusion = f32[640,320]{1,0:T(8,128)S(1)} fusion(s32[512]{0:T(512)S(1)} %bitcast.139, f32[512,320]{1,0:T(8,128)} %copy.23, f32[]{:T(128)} %constant.77.clone.1), kind=kCustom, calls=%fused_computation.71 | custom fusion | flops 163840 | bytes 819712 | tf_op jit(solution)/shard_map/scatter-add | solution.py:85
  32.4 4.0 %scatter_fusion = f32[640,320]{1,0:T(8,128)S(1)} fusion(f32[640,320]{1,0:T(8,128)S(1)} %scatter_custom_fusion, s32[512]{0:T(512)S(1)} %bitcast.137, f32[512,320]{1,0:T(8,128)S(1)} %copy.24), kind=kCustom, calls=%fused_computation.9 | custom fusion | flops 163840 | bytes 1968128 | tf_op jit(solution)/shard_map/scatter-add | solution.py:85
  36.4 4.0 %scatter_fusion.1 = f32[640,320]{1,0:T(8,128)S(1)} fusion(f32[640,320]{1,0:T(8,128)S(1)} %scatter_fusion, s32[512]{0:T(512)S(1)} %bitcast.135, f32[512,320]{1,0:T(8,128)S(1)} %copy-done.6), kind=kCustom, calls=%fused_computation.10 | custom fusion | flops 163840 | bytes 1968128 | tf_op jit(solution)/shard_map/scatter-add | solution.py:85
  40.4 4.2 %scatter_fusion.2 = f32[640,320]{1,0:T(8,128)S(1)} fusion(f32[640,320]{1,0:T(8,128)S(1)} %scatter_fusion.1, s32[512]{0:T(512)S(1)} %bitcast.133, f32[512,320]{1,0:T(8,128)S(1)} %copy-done.7), kind=kCustom, calls=%fused_computation.11 | custom fusion | flops 163840 | bytes 1968128 | tf_op jit(solution)/shard_map/scatter-add | solution.py:85
  44.6 4.0 %scatter_fusion.3 = f32[640,320]{1,0:T(8,128)S(1)} fusion(f32[640,320]{1,0:T(8,128)S(1)} %scatter_fusion.2, s32[512]{0:T(512)S(1)} %bitcast.131, f32[512,320]{1,0:T(8,128)S(1)} %copy-done.8), kind=kCustom, calls=%fused_computation.12 | custom fusion | flops 163840 | bytes 1968128 | tf_op jit(solution)/shard_map/scatter-add | solution.py:85
  48.6 4.0 %scatter_fusion.4 = f32[640,320]{1,0:T(8,128)S(1)} fusion(f32[640,320]{1,0:T(8,128)S(1)} %scatter_fusion.3, s32[512]{0:T(512)S(1)} %bitcast.129, f32[512,320]{1,0:T(8,128)S(1)} %copy-done.9), kind=kCustom, calls=%fused_computation.13 | custom fusion | flops 163840 | bytes 1968128 | tf_op jit(solution)/shard_map/scatter-add | solution.py:85
  52.6 0.3 copy.29
  52.9 0.7 fusion.119
  53.6 4.9 %collective-permute-start.2 = (bf16[64,320]{0,1:T(8,128)(2,1)S(1)}, bf16[64,320]{0,1:T(8,128)(2,1)S(1)}, u32[]{:S(2)}, u32[]{:S(2)}) collective-permute-start(bf16[64,320]{0,1:T(8,128)(2,1)S(1)} %get-tuple-element.34), channel_id=1, source_target_pairs={{0,1},{1,2},{2,3},{3,4},{4,5},{5,6},{6,7},{7,8},{8,9},{9,10},{10,1... | collective-permute-start | bytes 122888 | tf_op jit(solution)/shard_map/ppermute | solution.py:25
  58.5 1.9 %collective-permute-start.3 = (bf16[64,320]{0,1:T(8,128)(2,1)}, bf16[64,320]{0,1:T(8,128)(2,1)}, u32[]{:S(2)}, u32[]{:S(2)}) collective-permute-start(bf16[64,320]{0,1:T(8,128)(2,1)} %get-tuple-element.33), channel_id=1, source_target_pairs={{1,0},{2,1},{3,2},{4,3},{5,4},{6,5},{7,6},{8,7},{9,8},{10,9},{11,1... | collective-permute-start | bytes 122888 | tf_op jit(solution)/shard_map/ppermute | solution.py:25
  60.5 0.6 fusion.121
  61.1 1.3 convolution_multiply_fusion.13
  62.3 0.3 fusion.9
  62.7 0.3 fusion.8
  63.0 0.3 fusion.7
  63.3 0.3 fusion.6
  63.7 0.3 fusion.5
  64.0 1.2 fusion.4
  65.2 1.1 slice.265
  66.4 1.7 scatter-add.58
  68.2 1.1 slice_add_fusion
  69.3 1.8 scatter-add.59
  71.1 2.1 %fusion.22 = bf16[512,320]{0,1:T(8,128)(2,1)S(1)} fusion(bf16[320,320]{1,0:T(8,128)(2,1)S(1)} %copy-done, f32[512,320]{0,1:T(8,128)} %scatter-add.59, f32[512,320]{0,1:T(8,128)} %fusion.4, bf16[512,320]{0,1:T(8,128)(2,1)S(1)} %copy-done.1, bf16[512,320]{0,1:T(8,128)(2,1)} %param.21, f32[512]{0:T(512)} %bitcast.141, f32[512]{0:T(512)S(1)} %bitcast.114, ...), kind=kOutput, calls=%fused_computation.67 | convolution fusion | flops 211353600 | bytes 3117056 | tf_op jit(solution)/shard_map/dot_general | solution.py:29
  73.3 0.9 convolution_convert_fusion
  74.5 3.7 %collective-permute-start = (bf16[64,320]{1,0:T(8,128)(2,1)S(1)}, bf16[64,320]{1,0:T(8,128)(2,1)S(1)}, u32[]{:S(2)}, u32[]{:S(2)}) collective-permute-start(bf16[64,320]{1,0:T(8,128)(2,1)S(1)} %get-tuple-element.35), channel_id=1, source_target_pairs={{0,1},{1,2},{2,3},{3,4},{4,5},{5,6},{6,7},{7,8},{8,9},{9,10},{10,1... | collective-permute-start | bytes 122888 | tf_op jit(solution)/shard_map/ppermute | solution.py:16
  78.2 2.1 %collective-permute-start.1 = (bf16[64,320]{1,0:T(8,128)(2,1)S(1)}, bf16[64,320]{1,0:T(8,128)(2,1)S(1)}, u32[]{:S(2)}, u32[]{:S(2)}) collective-permute-start(bf16[64,320]{1,0:T(8,128)(2,1)S(1)} %get-tuple-element.36), channel_id=1, source_target_pairs={{1,0},{2,1},{3,2},{4,3},{5,4},{6,5},{7,6},{8,7},{9,8},{10,9},{11,1... | collective-permute-start | bytes 122888 | tf_op jit(solution)/shard_map/ppermute | solution.py:17
  80.6 0.4 convolution_multiply_fusion.21
  81.0 0.4 fusion.18
  81.3 0.4 fusion.17
  81.7 0.4 fusion.16
  82.1 0.4 fusion.15
  82.5 0.4 fusion.14
  82.9 0.4 fusion.13
  83.3 1.3 fusion.12
  84.9 2.6 %gather_fusion.1 = bf16[512,320]{1,0:T(8,128)(2,1)} fusion(bf16[640,320]{1,0:T(8,128)(2,1)S(1)} %pad_maximum_fusion, s32[1024]{0:T(1024)S(1)} %pad_clamp_fusion.6), kind=kCustom, calls=%fused_computation.1 | custom fusion | bytes 657408 | tf_op jit(solution)/shard_map/gather | solution.py:65
  87.4 2.6 %gather_fusion.2 = bf16[512,320]{1,0:T(8,128)(2,1)} fusion(bf16[640,320]{1,0:T(8,128)(2,1)S(1)} %pad_maximum_fusion, s32[1024]{0:T(1024)S(1)} %pad_clamp_fusion.5), kind=kCustom, calls=%fused_computation.2 | custom fusion | bytes 657408 | tf_op jit(solution)/shard_map/gather | solution.py:65
  90.0 2.6 %gather_fusion.3 = bf16[512,320]{1,0:T(8,128)(2,1)} fusion(bf16[640,320]{1,0:T(8,128)(2,1)S(1)} %pad_maximum_fusion, s32[1024]{0:T(1024)S(1)} %pad_clamp_fusion.4), kind=kCustom, calls=%fused_computation.3 | custom fusion | bytes 657408 | tf_op jit(solution)/shard_map/gather | solution.py:65
  92.6 2.6 %gather_fusion.4 = bf16[512,320]{1,0:T(8,128)(2,1)} fusion(bf16[640,320]{1,0:T(8,128)(2,1)S(1)} %pad_maximum_fusion, s32[1024]{0:T(1024)S(1)} %pad_clamp_fusion.3), kind=kCustom, calls=%fused_computation.4 | custom fusion | bytes 657408 | tf_op jit(solution)/shard_map/gather | solution.py:65
  95.1 2.6 %gather_fusion.5 = bf16[512,320]{1,0:T(8,128)(2,1)} fusion(bf16[640,320]{1,0:T(8,128)(2,1)S(1)} %pad_maximum_fusion, s32[1024]{0:T(1024)S(1)} %pad_clamp_fusion.2), kind=kCustom, calls=%fused_computation.5 | custom fusion | bytes 657408 | tf_op jit(solution)/shard_map/gather | solution.py:65
  97.7 2.6 %gather_fusion.6 = bf16[512,320]{1,0:T(8,128)(2,1)} fusion(bf16[640,320]{1,0:T(8,128)(2,1)S(1)} %pad_maximum_fusion, s32[1024]{0:T(1024)S(1)} %pad_clamp_fusion.1), kind=kCustom, calls=%fused_computation.6 | custom fusion | bytes 657408 | tf_op jit(solution)/shard_map/gather | solution.py:65
  100.3 1.5 convolution_add_fusion.5
  101.9 0.5 convolution_add_fusion.4
  102.4 0.5 convolution_add_fusion.3
  102.9 0.5 convolution_add_fusion.2
  103.4 0.5 convolution_add_fusion.1
  103.9 3.8 %gather_fusion = bf16[512,128]{1,0:T(8,128)(2,1)S(1)} fusion(bf16[16384,128]{1,0:T(8,128)(2,1)} %all-gather.3.cloned.1.call-done, s32[1024]{0:T(1024)S(1)} %pad_clamp_fusion.7), kind=kCustom, calls=%fused_computation | custom fusion | bytes 264192 | tf_op jit(solution)/shard_map/gather | solution.py:69
  107.7 2.3 %convolution_add_fusion.6 = f32[512,320]{0,1:T(8,128)} fusion(bf16[128,320]{0,1:T(8,128)(2,1)S(1)} %copy-done.19, bf16[512,320]{0,1:T(8,128)(2,1)} %param.20, bf16[512,128]{1,0:T(8,128)(2,1)S(1)} %gather_fusion, pred[512]{0:T(512)(128)(4,1)S(1)} %broadcast_compare_fusion.1), kind=kOutput, calls=%fused_computation.63 | convolution fusion | flops 42336256 | bytes 1196544 | tf_op jit(solution)/shard_map/dot_general | solution.py:71
  110.0 2.6 %fusion.20 = bf16[512,320]{0,1:T(8,128)(2,1)} fusion(bf16[320,320]{1,0:T(8,128)(2,1)S(1)} %copy-done, f32[512,320]{0,1:T(8,128)} %convolution_add_fusion.6, f32[512,320]{0,1:T(8,128)S(1)} %convolution_add_fusion.1, bf16[512,320]{0,1:T(8,128)(2,1)S(1)} %copy-done.2, bf16[512,320]{1,0:T(8,128)(2,1)S(1)} %copy-done.17, pred[512]{0:T(512)(128)(4,1)S(1)} %copy-done.46, ...), kind=kOutput, calls=%fused_computation.65 | convolution fusion | flops 211025920 | bytes 2853376 | tf_op jit(solution)/shard_map/dot_general | solution.py:73
  112.6 65.0 %all-gather.5.cloned.1.call-done = bf16[32768,128]{1,0:T(8,128)(2,1)} async-done(((bf16[512,128]{1,0:T(8,128)(2,1)}), bf16[32768,128]{1,0:T(8,128)(2,1)}) %all-gather.5.cloned.1.call-update) | async-done | bytes 8388624 | tf_op jit(solution)/shard_map/all_gather | solution.py:100
  177.5 5.8 %gather_fusion.7 = bf16[256,128]{1,0:T(8,128)(2,1)} fusion(bf16[32768,128]{1,0:T(8,128)(2,1)} %all-gather.5.cloned.1.call-done, s32[1024]{0:T(1024)S(1)} %pad_clamp_fusion), kind=kCustom, calls=%fused_computation.7 | custom fusion | bytes 132096 | tf_op jit(solution)/shard_map/gather | solution.py:101
  (129 shorter events, 1.2 us)
Async XLA Ops:
  7.2 63.9 %copy-start = (bf16[320,320]{1,0:T(8,128)(2,1)S(1)}, bf16[320,320]{1,0:T(8,128)(2,1)}, u32[]{:S(2)}) copy-start(bf16[320,320]{1,0:T(8,128)(2,1)} %param.25) | copy-start | bytes 614404
  7.2 4.3 %copy-start.1 = (bf16[512,320]{0,1:T(8,128)(2,1)S(1)}, bf16[512,320]{0,1:T(8,128)(2,1)}, u32[]{:S(2)}) copy-start(bf16[512,320]{0,1:T(8,128)(2,1)} %param.19) | copy-start | bytes 983044
  7.2 4.3 %copy-start.4 = (bf16[6,320,320]{2,1,0:T(8,128)(2,1)S(1)}, bf16[6,320,320]{2,1,0:T(8,128)(2,1)}, u32[]{:S(2)}) copy-start(bf16[6,320,320]{2,1,0:T(8,128)(2,1)} %param.24) | copy-start | bytes 3686404
  7.2 96.7 %all-gather.3.cloned.1.call-start = ((), (), s32[]{:S(2)}) async-start(), calls=%async_computation | async-start | bytes 4259840 | tf_op jit(solution)/shard_map/all_gather | solution.py:68
  7.9 169.6 %all-gather.5.cloned.1.call-start = ((), (), s32[]{:S(2)}) async-start(), calls=%async_computation.1 | async-start | bytes 8519680 | tf_op jit(solution)/shard_map/all_gather | solution.py:100
  8.8 2.7 %copy-start.41 = (pred[512]{0:T(512)(128)(4,1)}, pred[512]{0:T(512)(128)(4,1)S(1)}, u32[]{:S(2)}) copy-start(pred[512]{0:T(512)(128)(4,1)S(1)} %get-tuple-element.31) | copy-start | bytes 1540
  8.8 2.7 %copy-start.43 = (pred[512]{0:T(512)(128)(4,1)}, pred[512]{0:T(512)(128)(4,1)S(1)}, u32[]{:S(2)}) copy-start(pred[512]{0:T(512)(128)(4,1)S(1)} %get-tuple-element.32) | copy-start | bytes 1540
  8.8 5.2 %copy-start.39 = (pred[512]{0:T(512)(128)(4,1)}, pred[512]{0:T(512)(128)(4,1)S(1)}, u32[]{:S(2)}) copy-start(pred[512]{0:T(512)(128)(4,1)S(1)} %get-tuple-element.30) | copy-start | bytes 1540
  8.8 8.7 %copy-start.37 = (pred[512]{0:T(512)(128)(4,1)}, pred[512]{0:T(512)(128)(4,1)S(1)}, u32[]{:S(2)}) copy-start(pred[512]{0:T(512)(128)(4,1)S(1)} %get-tuple-element.29) | copy-start | bytes 1540
  8.8 12.1 %copy-start.35 = (pred[512]{0:T(512)(128)(4,1)}, pred[512]{0:T(512)(128)(4,1)S(1)}, u32[]{:S(2)}) copy-start(pred[512]{0:T(512)(128)(4,1)S(1)} %get-tuple-element.28) | copy-start | bytes 1540
  8.8 15.6 %copy-start.45 = (pred[512]{0:T(512)(128)(4,1)}, pred[512]{0:T(512)(128)(4,1)S(1)}, u32[]{:S(2)}) copy-start(pred[512]{0:T(512)(128)(4,1)S(1)} %get-tuple-element.27) | copy-start | bytes 1540
  22.1 5.7 %copy-start.21 = (s32[512,6]{0,1:T(8,128)S(1)}, s32[512,6]{0,1:T(8,128)}, u32[]{:S(2)}) copy-start(s32[512,6]{0,1:T(8,128)} %param.29) | copy-start | bytes 36868
  27.9 8.5 %copy-start.28 = (s32[512,1]{0,1:T(1,128)}, s32[512,1]{0,1:T(1,128)S(1)}, u32[]{:S(2)}) copy-start(s32[512,1]{0,1:T(1,128)S(1)} %get-tuple-element.41) | copy-start | bytes 6148
  27.9 8.5 %copy-start.31 = (s32[512,1]{0,1:T(1,128)}, s32[512,1]{0,1:T(1,128)S(1)}, u32[]{:S(2)}) copy-start(s32[512,1]{0,1:T(1,128)S(1)} %get-tuple-element.42) | copy-start | bytes 6148
  27.9 8.4 %copy-start.26 = (s32[512,1]{0,1:T(1,128)}, s32[512,1]{0,1:T(1,128)S(1)}, u32[]{:S(2)}) copy-start(s32[512,1]{0,1:T(1,128)S(1)} %get-tuple-element.40) | copy-start | bytes 6148
  27.9 12.4 %copy-start.24 = (s32[512,1]{0,1:T(1,128)}, s32[512,1]{0,1:T(1,128)S(1)}, u32[]{:S(2)}) copy-start(s32[512,1]{0,1:T(1,128)S(1)} %get-tuple-element.39) | copy-start | bytes 6148
  27.9 16.6 %copy-start.22 = (s32[512,1]{0,1:T(1,128)}, s32[512,1]{0,1:T(1,128)S(1)}, u32[]{:S(2)}) copy-start(s32[512,1]{0,1:T(1,128)S(1)} %get-tuple-element.38) | copy-start | bytes 6148
  32.3 4.0 %copy-start.6 = (f32[512,320]{1,0:T(8,128)S(1)}, f32[512,320]{1,0:T(8,128)}, u32[]{:S(2)}) copy-start(f32[512,320]{1,0:T(8,128)} %copy.25) | copy-start | bytes 1966084
  36.4 4.0 %copy-start.7 = (f32[512,320]{1,0:T(8,128)S(1)}, f32[512,320]{1,0:T(8,128)}, u32[]{:S(2)}) copy-start(f32[512,320]{1,0:T(8,128)} %copy.26) | copy-start | bytes 1966084
  40.4 4.2 %copy-start.8 = (f32[512,320]{1,0:T(8,128)S(1)}, f32[512,320]{1,0:T(8,128)}, u32[]{:S(2)}) copy-start(f32[512,320]{1,0:T(8,128)} %copy.27) | copy-start | bytes 1966084
  44.6 4.0 %copy-start.9 = (f32[512,320]{1,0:T(8,128)S(1)}, f32[512,320]{1,0:T(8,128)}, u32[]{:S(2)}) copy-start(f32[512,320]{1,0:T(8,128)} %copy.28) | copy-start | bytes 1966084
  52.5 7.9 %copy-start.30 = (f32[8,512]{1,0:T(8,128)S(1)}, f32[8,512]{1,0:T(8,128)}, u32[]{:S(2)}) copy-start(f32[8,512]{1,0:T(8,128)} %param.22) | copy-start | bytes 49156
  52.9 9.5 %copy-start.3 = (bf16[8,320,320]{2,1,0:T(8,128)(2,1)S(1)}, bf16[8,320,320]{2,1,0:T(8,128)(2,1)}, u32[]{:S(2)}) copy-start(bf16[8,320,320]{2,1,0:T(8,128)(2,1)} %param.23) | copy-start | bytes 4915204
  53.6 12.7 %collective-permute-start.2 = (bf16[64,320]{0,1:T(8,128)(2,1)S(1)}, bf16[64,320]{0,1:T(8,128)(2,1)S(1)}, u32[]{:S(2)}, u32[]{:S(2)}) collective-permute-start(bf16[64,320]{0,1:T(8,128)(2,1)S(1)} %get-tuple-element.34), channel_id=1, source_target_pairs={{0,1},{1,2},{2,3},{3,4},{4,5},{5,6},{6,7},{7,8},{8,9},{9,10},{10,1... | collective-permute-start | bytes 122888 | tf_op jit(solution)/shard_map/ppermute | solution.py:25
  58.5 9.7 %collective-permute-start.3 = (bf16[64,320]{0,1:T(8,128)(2,1)}, bf16[64,320]{0,1:T(8,128)(2,1)}, u32[]{:S(2)}, u32[]{:S(2)}) collective-permute-start(bf16[64,320]{0,1:T(8,128)(2,1)} %get-tuple-element.33), channel_id=1, source_target_pairs={{1,0},{2,1},{3,2},{4,3},{5,4},{6,5},{7,6},{8,7},{9,8},{10,9},{11,1... | collective-permute-start | bytes 122888 | tf_op jit(solution)/shard_map/ppermute | solution.py:25
  71.0 2.2 %copy-start.20 = (bf16[320,128]{1,0:T(8,128)(2,1)S(1)}, bf16[320,128]{1,0:T(8,128)(2,1)}, u32[]{:S(2)}) copy-start(bf16[320,128]{1,0:T(8,128)(2,1)} %param.27) | copy-start | bytes 245764
  71.0 3.2 %copy-start.2 = (bf16[512,320]{0,1:T(8,128)(2,1)S(1)}, bf16[512,320]{0,1:T(8,128)(2,1)}, u32[]{:S(2)}) copy-start(bf16[512,320]{0,1:T(8,128)(2,1)} %param.18) | copy-start | bytes 983044
  71.1 9.3 %copy-start.32 = (s32[512,1]{0,1:T(1,128)S(1)}, s32[512,1]{0,1:T(1,128)}, u32[]{:S(2)}) copy-start(s32[512,1]{0,1:T(1,128)} %copy-done.31) | copy-start | bytes 6148
  71.1 9.3 %copy-start.29 = (s32[512,1]{0,1:T(1,128)S(1)}, s32[512,1]{0,1:T(1,128)}, u32[]{:S(2)}) copy-start(s32[512,1]{0,1:T(1,128)} %copy-done.28) | copy-start | bytes 6148
  71.1 9.3 %copy-start.27 = (s32[512,1]{0,1:T(1,128)S(1)}, s32[512,1]{0,1:T(1,128)}, u32[]{:S(2)}) copy-start(s32[512,1]{0,1:T(1,128)} %copy-done.26) | copy-start | bytes 6148
  71.1 9.4 %copy-start.25 = (s32[512,1]{0,1:T(1,128)S(1)}, s32[512,1]{0,1:T(1,128)}, u32[]{:S(2)}) copy-start(s32[512,1]{0,1:T(1,128)} %copy-done.24) | copy-start | bytes 6148
  71.1 9.4 %copy-start.23 = (s32[512,1]{0,1:T(1,128)S(1)}, s32[512,1]{0,1:T(1,128)}, u32[]{:S(2)}) copy-start(s32[512,1]{0,1:T(1,128)} %copy-done.22) | copy-start | bytes 6148
  71.1 9.4 %copy-start.47 = (s32[256]{0:T(256)S(1)}, s32[256]{0:T(256)}, u32[]{:S(2)}) copy-start(s32[256]{0:T(256)} %param.31) | copy-start | bytes 3076
  71.1 9.4 %copy-start.33 = (s32[512]{0:T(512)S(1)}, s32[512]{0:T(512)}, u32[]{:S(2)}) copy-start(s32[512]{0:T(512)} %param.30) | copy-start | bytes 6148
  73.3 1.0 copy-start.18
  74.5 7.2 %copy-start.11 = (bf16[512,320]{1,0:T(8,128)(2,1)}, bf16[512,320]{1,0:T(8,128)(2,1)S(1)}, u32[]{:S(2)}) copy-start(bf16[512,320]{1,0:T(8,128)(2,1)S(1)} %copy.20) | copy-start | bytes 983044
  74.5 10.1 %collective-permute-start = (bf16[64,320]{1,0:T(8,128)(2,1)S(1)}, bf16[64,320]{1,0:T(8,128)(2,1)S(1)}, u32[]{:S(2)}, u32[]{:S(2)}) collective-permute-start(bf16[64,320]{1,0:T(8,128)(2,1)S(1)} %get-tuple-element.35), channel_id=1, source_target_pairs={{0,1},{1,2},{2,3},{3,4},{4,5},{5,6},{6,7},{7,8},{8,9},{9,10},{10,1... | collective-permute-start | bytes 122888 | tf_op jit(solution)/shard_map/ppermute | solution.py:16
  78.2 6.6 %collective-permute-start.1 = (bf16[64,320]{1,0:T(8,128)(2,1)S(1)}, bf16[64,320]{1,0:T(8,128)(2,1)S(1)}, u32[]{:S(2)}, u32[]{:S(2)}) collective-permute-start(bf16[64,320]{1,0:T(8,128)(2,1)S(1)} %get-tuple-element.36), channel_id=1, source_target_pairs={{1,0},{2,1},{3,2},{4,3},{5,4},{6,5},{7,6},{8,7},{9,8},{10,9},{11,1... | collective-permute-start | bytes 122888 | tf_op jit(solution)/shard_map/ppermute | solution.py:17
  82.5 0.8 copy-start.34
  82.9 1.9 copy-start.12
  97.7 2.6 %copy-start.5 = (bf16[6,320,320]{2,1,0:T(8,128)(2,1)S(1)}, bf16[6,320,320]{2,1,0:T(8,128)(2,1)}, u32[]{:S(2)}) copy-start(bf16[6,320,320]{2,1,0:T(8,128)(2,1)} %param.24) | copy-start | bytes 3686404
  97.7 2.6 %copy-start.10 = (f32[512,320]{0,1:T(8,128)S(1)}, f32[512,320]{0,1:T(8,128)}, u32[]{:S(2)}) copy-start(f32[512,320]{0,1:T(8,128)} %fusion.12) | copy-start | bytes 1966084
  97.7 2.6 %copy-start.44 = (pred[512]{0:T(512)(128)(4,1)S(1)}, pred[512]{0:T(512)(128)(4,1)}, u32[]{:S(2)}) copy-start(pred[512]{0:T(512)(128)(4,1)} %copy-done.43) | copy-start | bytes 1540
  97.7 4.1 %copy-start.42 = (pred[512]{0:T(512)(128)(4,1)S(1)}, pred[512]{0:T(512)(128)(4,1)}, u32[]{:S(2)}) copy-start(pred[512]{0:T(512)(128)(4,1)} %copy-done.41) | copy-start | bytes 1540
  100.3 1.6 copy-start.16
  100.3 2.1 %copy-start.15 = (bf16[512,320]{1,0:T(8,128)(2,1)S(1)}, bf16[512,320]{1,0:T(8,128)(2,1)}, u32[]{:S(2)}) copy-start(bf16[512,320]{1,0:T(8,128)(2,1)} %gather_fusion.3) | copy-start | bytes 983044
  100.3 2.1 %copy-start.40 = (pred[512]{0:T(512)(128)(4,1)S(1)}, pred[512]{0:T(512)(128)(4,1)}, u32[]{:S(2)}) copy-start(pred[512]{0:T(512)(128)(4,1)} %copy-done.39) | copy-start | bytes 1540
  101.9 1.0 copy-start.14
  101.9 1.0 copy-start.38
  102.4 1.0 copy-start.13
  102.4 1.0 copy-start.36
  103.4 4.3 %copy-start.19 = (bf16[128,320]{0,1:T(8,128)(2,1)S(1)}, bf16[128,320]{0,1:T(8,128)(2,1)}, u32[]{:S(2)}) copy-start(bf16[128,320]{0,1:T(8,128)(2,1)} %param.26) | copy-start | bytes 245764
  103.4 6.6 %copy-start.46 = (pred[512]{0:T(512)(128)(4,1)S(1)}, pred[512]{0:T(512)(128)(4,1)}, u32[]{:S(2)}) copy-start(pred[512]{0:T(512)(128)(4,1)} %copy-done.45) | copy-start | bytes 1540
  103.9 6.1 %copy-start.17 = (bf16[512,320]{1,0:T(8,128)(2,1)S(1)}, bf16[512,320]{1,0:T(8,128)(2,1)}, u32[]{:S(2)}) copy-start(bf16[512,320]{1,0:T(8,128)(2,1)} %gather_fusion.6) | copy-start | bytes 983044
Sparse Core Ops, SparseCore 0:
  10.8 83.2 all-gather.2
  96.9 80.5 all-gather.4
where the time goes:
time: 191 us; the launch traced here: 190 us
  waiting for transfers between devices  65.9 us (35%)
  local copies, waits for them, and re-layouts  43.3 us (23%)
  other arithmetic  26.6 us (14%)
  matrix products  26.6 us (14%)
  between operations  15 us (8%)
  starting transfers between devices  12.8 us (7%)
    all_gather x1, waiting for transfers between devices, on_device(): gathered_load = lax.all_gather(traction, 'elem', axis=0, tiled=True)  65 us
    scatter-add x6, other arithmetic, on_device(): collected = collected.at[local_index[:, face]].add(pushed)  24.4 us
    gather x6, local copies, waits for them, and re-layouts, on_device(): extended[local_index[:, face]]  15.4 us
    dot_general x14, matrix products, times_transposed(): lax.dot_general(left, right, (((1,), (1,)), ((), ())), preferred_element_...  13.6 us
    mul x6, local copies, waits for them, and re-layouts, on_device(): times_transposed(adjoint, face_tiles[face])  11.6 us
    ppermute x2, starting transfers between devices, shifted(): return lax.ppermute(block, axis, route)  6.85 us
    gather x1, local copies, waits for them, and re-layouts, on_device(): wall_load = gathered_load[wall_target]  5.8 us
    dot_general x8, matrix products, on_device(): jnp.dot(state, basis_tiles[level], preferred_element_type=jnp.float32)  3.93 us
  transfers between devices with their start and end apart: 6, of which 2 were waited for; matrix products, arithmetic and copies ran while one was open for 48% of the time, Pallas kernels for 0%

commit v1 on v0

v1 whole, which is shorter than its diff:
```python
import jax
import jax.numpy as jnp
from jax import lax
from jax.experimental import pallas as pl
from jax.experimental.pallas import tpu as pltpu
from jax.sharding import PartitionSpec as P

HALO = 64
BLOCK = 128
MAIN = 256
CAP = 8
F32 = jnp.float32
BF16 = jnp.bfloat16
NT = (((1,), (1,)), ((), ()))


def columns_of(rows, count):
    padded = jnp.concatenate([rows] + [jnp.zeros_like(rows)] * (128 // rows.shape[0] - 1), axis=0)
    return jnp.transpose(padded)


def diagonal_kernel(
    state_ref,
    adjoint_ref,
    metric_ref,
    basis_ref,
    wall_node_ref,
    wall_target_ref,
    diag_ref,
    diag_t_ref,
    srow_ref,
    scol_ref,
    x_ref,
    w_ref,
):
    elems, width = state_ref.shape
    count = basis_ref.shape[0]
    tail = width - MAIN
    factors = columns_of(metric_ref[...], elems)

    def scaled_into(value_ref):
        value = value_ref[...].astype(F32)
        main, rest = value[:, :MAIN], value[:, MAIN:]
        tails = []
        for k in range(count):
            x_ref[:, k * MAIN : (k + 1) * MAIN] = (main * factors[:, k : k + 1]).astype(BF16)
            tails.append((rest * factors[:, k : k + 1]).astype(BF16))
        x_ref[:, count * MAIN :] = jnp.concatenate(tails, axis=1)

    scaled_into(state_ref)
    for k in range(count):
        w_ref[k * MAIN : (k + 1) * MAIN, :] = basis_ref[k, :MAIN, :]
        w_ref[count * MAIN + k * tail : count * MAIN + (k + 1) * tail, :] = basis_ref[k, MAIN:, :]
    diag_ref[...] = jnp.dot(x_ref[...], w_ref[...], preferred_element_type=F32)

    scaled_into(adjoint_ref)
    total = lax.dot_general(
        x_ref[:, count * MAIN :],
        jnp.concatenate([basis_ref[k, :, MAIN:] for k in range(count)], axis=1),
        NT,
        preferred_element_type=F32,
    )
    for k in range(count):
        total += lax.dot_general(
            x_ref[:, k * MAIN : (k + 1) * MAIN],
            basis_ref[k, :, :MAIN],
            NT,
            preferred_element_type=F32,
        )
    diag_t_ref[...] = total

    def slots(device_row, order_row):
        n = device_row.shape[1]
        device_col = jnp.transpose(jnp.broadcast_to(device_row, (128, n)))[:, :1]
        order_col = jnp.transpose(jnp.broadcast_to(order_row, (128, n)))[:, :1]
        same = device_col == device_row
        before = jnp.where(same & (order_col < order_row), 1.0, 0.0)
        after = jnp.where(same & (order_row < order_col), 1.0, 0.0)
        row = device_row * CAP + jnp.sum(before, axis=0, keepdims=True)
        col = device_col * CAP + jnp.sum(after, axis=1, keepdims=True)
        return row, col

    nodes = wall_target_ref.shape[1]
    target = wall_target_ref[...]
    node_order = lax.broadcasted_iota(jnp.int32, (1, nodes), 1).astype(F32)
    node_row, node_col = slots((target // elems).astype(F32), node_order)
    node = wall_node_ref[...]
    owner = jnp.where(node >= 0, node // nodes, -1).astype(F32)
    elem_row, elem_col = slots(owner, node.astype(F32))
    srow_ref[...] = jnp.zeros(srow_ref.shape, F32)
    srow_ref[0:1, :] = elem_row
    srow_ref[1:2, :nodes] = node_row
    scol_ref[0] = elem_col
    scol_ref[1, :nodes] = node_col


def faces_kernel(
    state_ref,
    adjoint_ref,
    right_ref,
    source_ref,
    metric_ref,
    faces_ref,
    precond_ref,
    traction_tile_ref,
    mode_ref,
    neighbors_ref,
    code_ref,
    before_ref,
    after_ref,
    diag_ref,
    diag_t_ref,
    srow_ref,
    rest_ref,
    new_adjoint_ref,
    send_ref,
    x_ref,
    w_ref,
):
    elems, width = state_ref.shape
    count = faces_ref.shape[0]
    tail = width - MAIN
    offset = width + tail
    blocks = elems // BLOCK

    def window(value_ref, start, b):
        low, high = b * BLOCK - HALO, b * BLOCK + BLOCK + HALO
        parts = []
        if low < 0:
            parts.append(before_ref[:, start : start + width])
        parts.append(value_ref[max(low, 0) : min(high, elems), :])
        if high > elems:
            parts.append(after_ref[:, start : start + width])
        return parts[0] if len(parts) == 1 else jnp.concatenate(parts, axis=0)

    def place(b, gathered):
        rows = slice(b * BLOCK, (b + 1) * BLOCK)
        tails = []
        for f in range(count):
            one = gathered[f * BLOCK : (f + 1) * BLOCK, :]
            x_ref[rows, f * MAIN : (f + 1) * MAIN] = one[:, :MAIN]
            tails.append(one[:, MAIN:])
        x_ref[rows, count * MAIN :] = jnp.concatenate(tails, axis=1)

    own = code_ref[...].astype(F32)
    pad = jnp.zeros((elems, 128 - own.shape[1]), F32)
    own_rows = jnp.transpose(jnp.concatenate([own, pad], axis=1))[:8, :]
    zero_side = jnp.zeros((HALO, 2 * HALO), F32)
    low_rows = jnp.transpose(
        jnp.concatenate([before_ref[:, width : width + tail].astype(F32), zero_side[:, :HALO]], axis=1)
    )[:8, :]
    high_rows = jnp.transpose(
        jnp.concatenate([after_ref[:, width : width + tail].astype(F32), zero_side[:, :HALO]], axis=1)
    )[:8, :]
    codes = jnp.concatenate([low_rows, own_rows, high_rows], axis=1)
    codes = jnp.where(codes == 0.0, -1000.0, codes)
    span = BLOCK + 2 * HALO
    lane = lax.broadcasted_iota(jnp.int32, (8, span), 1).astype(F32)
    place_row = lax.broadcasted_iota(jnp.int32, (BLOCK, span), 0).astype(F32)
    place_lane = lax.broadcasted_iota(jnp.int32, (BLOCK, span), 1)
    for b in range(blocks):
        targets = codes[:, b * BLOCK : b * BLOCK + span] + lane - (2.0 * HALO + 1.0)
        hot = jnp.concatenate(
            [
                jnp.where(place_row == targets[f : f + 1, :], 1.0, 0.0).astype(BF16)
                for f in range(count)
            ],
            axis=0,
        )
        place(
            b,
            jnp.dot(hot, window(adjoint_ref, offset, b), preferred_element_type=F32).astype(BF16),
        )
    total = lax.dot_general(
        x_ref[:, count * MAIN :],
        jnp.concatenate([faces_ref[f, :, MAIN:] for f in range(count)], axis=1),
        NT,
        preferred_element_type=F32,
    )
    for f in range(count):
        total += lax.dot_general(
            x_ref[:, f * MAIN : (f + 1) * MAIN],
            faces_ref[f, :, :MAIN],
            NT,
            preferred_element_type=F32,
        )
    factor = columns_of(metric_ref[...], elems)[:, :1]
    residual_t = (source_ref[...].astype(F32) - (diag_t_ref[...] + total)).astype(BF16)
    update_t = lax.dot_general(residual_t, precond_ref[...], NT, preferred_element_type=F32)
    new_adjoint = (adjoint_ref[...].astype(F32) + update_t / factor).astype(BF16)
    new_adjoint_ref[...] = new_adjoint
    traction = jnp.dot(new_adjoint, traction_tile_ref[...], preferred_element_type=F32).astype(BF16)

    slots = elems
    elem_hot = jnp.where(
        lax.broadcasted_iota(jnp.int32, (slots, elems), 0).astype(F32) == srow_ref[0:1, :], 1.0, 0.0
    ).astype(BF16)
    nodes = mode_ref.shape[0]
    node_hot = jnp.where(
        lax.broadcasted_iota(jnp.int32, (slots, nodes), 0).astype(F32) == srow_ref[1:2, :nodes],
        1.0,
        0.0,
    ).astype(BF16)
    out_modes = jnp.dot(node_hot, mode_ref[...], preferred_element_type=F32)
    out_traction = jnp.dot(elem_hot, traction, preferred_element_type=F32)
    lanes = out_modes.shape[1]
    send_ref[...] = (
        jnp.concatenate(
            [
                out_modes.reshape(slots // CAP, CAP, lanes),
                out_traction.reshape(slots // CAP, CAP, lanes),
            ],
            axis=1,
        )
        .reshape(2 * slots, lanes)
        .astype(BF16)
    )

    for b in range(blocks):
        local = neighbors_ref[b * BLOCK : (b + 1) * BLOCK, :]
        hot = jnp.concatenate(
            [
                jnp.where(place_lane == local[:, f : f + 1] - b * BLOCK, 1.0, 0.0).astype(BF16)
                for f in range(count)
            ],
            axis=0,
        )
        place(b, jnp.dot(hot, window(state_ref, 0, b), preferred_element_type=F32).astype(BF16))
    for f in range(count):
        w_ref[f * MAIN : (f + 1) * MAIN, :] = faces_ref[f, :MAIN, :]
        w_ref[count * MAIN + f * tail : count * MAIN + (f + 1) * tail, :] = faces_ref[f, MAIN:, :]
    coupled = jnp.dot(x_ref[...], w_ref[...], preferred_element_type=F32)
    rest_ref[...] = right_ref[...].astype(F32) - (diag_ref[...] + coupled)


def finish_kernel(
    state_ref,
    metric_ref,
    precond_ref,
    wall_tile_ref,
    rest_ref,
    scol_ref,
    received_ref,
    new_state_ref,
    wall_load_ref,
):
    elems = state_ref.shape[0]
    nodes = wall_load_ref.shape[0]
    slots = elems
    lanes = received_ref.shape[1]
    received = received_ref[...].astype(F32).reshape(slots // CAP, 2 * CAP, lanes)
    modes = received[:, :CAP, :].reshape(slots, lanes).astype(BF16)
    traction = received[:, CAP:, :].reshape(slots, lanes).astype(BF16)
    elem_hot = jnp.where(
        lax.broadcasted_iota(jnp.int32, (elems, slots), 1).astype(F32) == scol_ref[0], 1.0, 0.0
    ).astype(BF16)
    node_hot = jnp.where(
        lax.broadcasted_iota(jnp.int32, (nodes, slots), 1).astype(F32) == scol_ref[1, :nodes],
        1.0,
        0.0,
    ).astype(BF16)
    wall_load_ref[...] = jnp.dot(node_hot, traction, preferred_element_type=F32).astype(BF16)
    wall_modes = jnp.dot(elem_hot, modes, preferred_element_type=F32).astype(BF16)
    forcing = jnp.dot(wall_modes, wall_tile_ref[...], preferred_element_type=F32)
    residual = (rest_ref[...] + forcing).astype(BF16)
    update = jnp.dot(residual, precond_ref[...], preferred_element_type=F32)
    factor = columns_of(metric_ref[...], elems)[:, :1]
    new_state_ref[...] = (state_ref[...].astype(F32) + update / factor).astype(BF16)


def call(kernel, outs, scratch, flops, args, name):
    spec = pl.BlockSpec(memory_space=pltpu.VMEM)
    size = sum(a.size * a.dtype.itemsize for a in args)
    return pl.pallas_call(
        kernel,
        out_shape=outs,
        in_specs=[spec] * len(args),
        out_specs=[spec] * len(outs),
        scratch_shapes=scratch,
        compiler_params=pltpu.CompilerParams(vmem_limit_bytes=40 * 1024 * 1024),
        cost_estimate=pl.CostEstimate(flops=flops, bytes_accessed=size, transcendentals=0),
        name=name,
    )(*args)


def on_device(
    state,
    adjoint,
    right_side,
    source,
    metric,
    basis_tiles,
    face_tiles,
    precond,
    wall_tile,
    traction_tile,
    mode_rows,
    neighbors,
    wall_node,
    wall_target,
):
    elems, width = state.shape
    nodes, lanes = mode_rows.shape
    geo, faces = basis_tiles.shape[0], face_tiles.shape[0]
    devices = lax.axis_size("elem")
    tail = width - MAIN
    base = lax.axis_index("elem") * elems
    linked = neighbors >= 0
    element = base + lax.broadcasted_iota(jnp.int32, neighbors.shape, 0)
    code = jnp.where(linked, neighbors - element + (HALO + 1), 0).astype(BF16)
    local = jnp.where(linked, neighbors - base + HALO, -1)

    def packed(rows):
        side = jnp.pad(code[rows], ((0, 0), (0, tail - faces)))
        return jnp.concatenate(
            [state[rows], side, adjoint[rows], jnp.zeros((HALO, tail), BF16)], axis=1
        )

    up = [(i, i + 1) for i in range(devices - 1)]
    down = [(j, i) for i, j in up]
    before = lax.ppermute(packed(slice(elems - HALO, elems)), "elem", up)
    after = lax.ppermute(packed(slice(0, HALO)), "elem", down)

    sds = jax.ShapeDtypeStruct
    wide = sds((elems, width), F32)
    narrow = sds((elems, width), BF16)
    diag, diag_t, srow, scol = call(
        diagonal_kernel,
        [wide, wide, sds((8, elems), F32), sds((2, elems, 1), F32)],
        [pltpu.VMEM((elems, geo * width), BF16), pltpu.VMEM((geo * width, width), BF16)],
        4 * geo * elems * width * width,
        (
            state,
            adjoint,
            metric,
            basis_tiles,
            wall_node.reshape(1, elems),
            wall_target.reshape(1, nodes),
        ),
        "diagonal",
    )
    rest, new_adjoint, send = call(
        faces_kernel,
        [wide, narrow, sds((2 * elems, lanes), BF16)],
        [pltpu.VMEM((elems, faces * width), BF16), pltpu.VMEM((faces * width, width), BF16)],
        4 * (faces + 1) * elems * width * width,
        (
            state,
            adjoint,
            right_side,
            source,
            metric,
            face_tiles,
            precond,
            traction_tile,
            mode_rows,
            local,
            code,
            before,
            after,
            diag,
            diag_t,
            srow,
        ),
        "faces",
    )
    received = lax.all_to_all(send, "elem", 0, 0, tiled=True)
    new_state, wall_load = call(
        finish_kernel,
        [narrow, sds((nodes, lanes), BF16)],
        [],
        4 * elems * width * width,
        (state, metric, precond, wall_tile, rest, scol, received),
        "finish",
    )
    return (new_state, new_adjoint, wall_load)


def solution(mesh):
    rows = P(("phase", "elem"), None)
    return jax.shard_map(
        on_device,
        mesh=mesh,
        in_specs=(
            rows,
            rows,
            rows,
            rows,
            P(None, "elem"),
            P("phase", None, None),
            P("phase", None, None),
            P("phase", None),
            P("phase", None),
            P("phase", None),
            rows,
            P("elem", None),
            P("elem"),
            P("elem"),
        ),
        out_specs=(rows, rows, rows),
        check_vma=False,
    )
```

time: 191 us -> 49.8 us (0.26)
  waiting for transfers between devices: 65.9 us -> 9.99 us
  local copies, waits for them, and re-layouts: 43.3 us -> 8.68 us
  matrix products: 26.6 us -> 0 us
  other arithmetic: 26.6 us -> 0.87 us
  between operations: 15 us -> 0.96 us
  Pallas kernels: 0 us -> 9.17 us
  starting transfers between devices: 12.8 us -> 19.8 us
    all_gather x2 -> x0, waiting for transfers between devices: 65 us -> none  [the longest x1 65 us: on_device(): gathered_load = lax.all_gather(traction, 'elem', axis=0, tiled=True)]
    dot_general x30 -> x0, matrix products: 26.6 us -> none  [the longest x14 13.6 us: times_transposed(): lax.dot_general(left, right, (((1,), (1,)), ((), ())), preferred_element_...]
    gather x8 -> x0, local copies, waits for them, and re-layouts: 25 us -> none  [the longest x6 15.4 us: on_device(): extended[local_index[:, face]]]
    scatter-add x6 -> x0, other arithmetic: 24.4 us -> none  [on_device(): collected = collected.at[local_index[:, face]].add(pushed)]
    all_to_all x0 -> x1, starting transfers between devices: none -> 12.9 us  [on_device(): received = lax.all_to_all(send, 'elem', 0, 0, tiled=True)]
    mul x6 -> x0, local copies, waits for them, and re-layouts: 11.6 us -> none  [on_device(): times_transposed(adjoint, face_tiles[face])]
    all_to_all x0 -> x1, waiting for transfers between devices: none -> 9.98 us  [on_device(): received = lax.all_to_all(send, 'elem', 0, 0, tiled=True)]
    pallas_call x0 -> x3, Pallas kernels: none -> 9.17 us  [call(): pl.pallas_call(kernel, out_shape=outs, in_specs=[spec] * len(args), out_s...]
  transfers between devices with their start and end apart: 6 -> 3, of which waited for: 2 -> 1; matrix products, arithmetic and copies ran while one was open for 48% -> 6% of each run, Pallas kernels for 0% -> 7%
where the time goes in v1:
time: 49.8 us; the launch traced here: 49.4 us
  starting transfers between devices  19.8 us (40%)
  waiting for transfers between devices  9.99 us (20%)
  Pallas kernels  9.17 us (18%)
  local copies, waits for them, and re-layouts  8.68 us (17%)
  between operations  0.96 us (2%)
  other arithmetic  0.87 us (2%)
    all_to_all x1, starting transfers between devices, on_device(): received = lax.all_to_all(send, 'elem', 0, 0, tiled=True)  12.9 us
    all_to_all x1, waiting for transfers between devices, on_device(): received = lax.all_to_all(send, 'elem', 0, 0, tiled=True)  9.98 us
    pallas_call x3, Pallas kernels, call(): pl.pallas_call(kernel, out_shape=outs, in_specs=[spec] * len(args), out_s...  9.17 us
    unnamed x33, local copies, waits for them, and re-layouts  8.09 us
    ppermute x1, starting transfers between devices, on_device(): before = lax.ppermute(packed(slice(elems - HALO, elems)), 'elem', up)  4.94 us
    ppermute x1, starting transfers between devices, on_device(): after = lax.ppermute(packed(slice(0, HALO)), 'elem', down)  1.92 us
  transfers between devices with their start and end apart: 3, of which 1 were waited for; matrix products, arithmetic and copies ran while one was open for 6% of the time, Pallas kernels for 7%

profile of v1, /device:TPU:1, one launch (start us, length us, event | category | flops | bytes accessed | tf_op | source)
XLA Modules:
  0.0 49.4 jit_solution(13847414363998513509)
XLA Ops:
  0.6 0.0 copy-start.12
  0.6 0.0 copy-start.9
  0.7 0.0 copy-start.10
  0.7 1.2 %copy.53.state_ref = bf16[512,320]{1,0:T(8,128)(2,1)S(1)} copy(bf16[512,320]{0,1:T(8,128)(2,1)} %param.14) | data formatting | bytes 655360 | tf_op args[0]
  1.9 1.2 %copy.50.adjoint_ref = bf16[512,320]{1,0:T(8,128)(2,1)S(1)} copy(bf16[512,320]{0,1:T(8,128)(2,1)} %param.15) | data formatting | bytes 655360 | tf_op args[1]
  3.1 0.7 %add_select_fusion = (s32[512,6]{0,1:T(8,128)S(1)}, s32[512,6]{0,1:T(8,128)S(1)}) fusion(s32[512,6]{0,1:T(8,128)} %param.25, s32[512]{0:T(512)S(1)} %iota_add_fusion, s32[]{:T(128)S(6)} %mul.3), kind=kLoop, calls=%fused_computation.12 | loop fusion | flops 18432 | bytes 38916 | tf_op jit(solution)/shard_map/jit(_where)/select_n | solution.py:310
  3.9 0.0 copy-start.5
  3.9 0.0 copy-start.7
  3.9 0.0 copy-start.8
  3.9 0.1 copy.42
  4.1 0.1 pad.16.clone
  4.2 0.1 fusion.8
  4.3 4.9 %collective-permute-start = (bf16[64,768]{1,0:T(8,128)(2,1)S(1)}, bf16[64,768]{1,0:T(8,128)(2,1)S(1)}, u32[]{:S(2)}, u32[]{:S(2)}) collective-permute-start(bf16[64,768]{1,0:T(8,128)(2,1)S(1)} %get-tuple-element.36), channel_id=1, source_target_pairs={{0,1},{1,2},{2,3},{3,4},{4,5},{5,6},{6,7},{7,8},{8,9},{9,10},{10,1... | collective-permute-start | bytes 294920 | tf_op jit(solution)/shard_map/ppermute | solution.py:321
  9.2 1.9 %collective-permute-start.1 = (bf16[64,768]{1,0:T(8,128)(2,1)S(1)}, bf16[64,768]{1,0:T(8,128)(2,1)S(1)}, u32[]{:S(2)}, u32[]{:S(2)}) collective-permute-start(bf16[64,768]{1,0:T(8,128)(2,1)S(1)} %get-tuple-element.35), channel_id=1, source_target_pairs={{1,0},{2,1},{3,2},{4,3},{5,4},{6,5},{7,6},{8,7},{9,8},{10,9},{11,1... | collective-permute-start | bytes 294920 | tf_op jit(solution)/shard_map/ppermute | solution.py:322
  11.1 0.0 copy-done.12
  11.2 0.1 copy.41
  11.3 0.2 copy.40
  11.5 0.0 copy-done.9
  11.5 0.2 copy.51.right_ref
  11.8 0.0 copy-done.10
  11.8 0.2 copy.52.source_ref
  12.0 0.0 copy-done.5
  12.0 0.0 copy-done.7
  12.0 0.0 copy-done.8
  12.0 0.0 copy-start.6
  12.1 1.5 %copy-done.6 = bf16[8,320,320]{2,1,0:T(8,128)(2,1)S(1)} copy-done((bf16[8,320,320]{2,1,0:T(8,128)(2,1)S(1)}, bf16[8,320,320]{2,1,0:T(8,128)(2,1)}, u32[]{:S(2)}) %copy-start.6) | copy-done | bytes 1638424
  13.6 0.0 copy-start
  13.6 0.0 copy-start.1
  13.6 0.0 copy-start.3
  13.6 0.0 copy-start.4
  13.6 3.3 %diagonal.1 = (f32[512,320]{1,0:T(8,128)S(1)}, f32[512,320]{1,0:T(8,128)S(1)}, f32[8,512]{1,0:T(8,128)S(1)}, f32[2,512,1]{2,1,0:T(8,128)S(1)}) custom-call(bf16[512,320]{1,0:T(8,128)(2,1)S(1)} %copy.53.state_ref, bf16[512,320]{1,0:T(8,128)(2,1)S(1)} %copy.50.adjoint_ref, f32[8,512]{1,0:T(8,128)S(1)} %copy-done.5, bf16[8,320,320]{2,1,0:T(8,128)(2,1)S(1)} %copy-done.6, ...), custom_call_target="tpu_custom_call" | custom-call | flops 1677721600 | bytes 2313216 | tf_op jit(solution)/shard_map/diagonal/pallas_call | solution.py:274
  16.9 0.0 collective-permute-done.before_ref
  16.9 0.0 collective-permute-done.1.after_ref
  16.9 0.0 copy-done
  16.9 0.0 copy-done.1
  17.0 0.0 copy-done.3
  17.0 0.0 copy-done.4
  17.0 0.0 copy-start.11
  17.0 4.8 %faces.1 = (f32[512,320]{1,0:T(8,128)S(1)}, bf16[512,320]{1,0:T(8,128)(2,1)S(1)}, bf16[1024,128]{1,0:T(8,128)(2,1)}) custom-call(bf16[512,320]{1,0:T(8,128)(2,1)S(1)} %copy.53.state_ref, bf16[512,320]{1,0:T(8,128)(2,1)S(1)} %copy.50.adjoint_ref, bf16[512,320]{1,0:T(8,128)(2,1)S(1)} %copy.51.right_ref, bf16[512,320]{1,0:T(8,128)(2,1)S(1)} %copy.52.source_ref, ...), custom_call_target="tpu_custom_call" | custom-call | flops 1468006400 | bytes 4450304 | tf_op jit(solution)/shard_map/faces/pallas_call | solution.py:274
  21.8 0.0 copy-start.2
  21.8 0.7 %copy-done.2 = bf16[512,320]{1,0:T(8,128)(2,1)} copy-done((bf16[512,320]{1,0:T(8,128)(2,1)}, bf16[512,320]{1,0:T(8,128)(2,1)S(1)}, u32[]{:S(2)}) %copy-start.2) | copy-done | bytes 327704
  22.6 12.9 %all-to-all-start = ((bf16[64,16,128]{2,1,0:T(8,128)(2,1)}), bf16[64,16,128]{2,1,0:T(8,128)(2,1)S(1)}, u32[]{:S(2)}, u32[]{:S(2)}) async-start(bf16[64,16,128]{2,1,0:T(8,128)(2,1)} %bitcast.2), calls=%async_computation | async-start | bytes 524288 | tf_op jit(solution)/shard_map/all_to_all | solution.py:367
  35.5 0.0 copy-done.11
  35.5 0.1 copy.54.wall_tile_ref
  35.6 1.9 %copy.56 = bf16[512,320]{0,1:T(8,128)(2,1)} copy(bf16[512,320]{1,0:T(8,128)(2,1)} %copy-done.2) | data formatting | bytes 655360
  37.5 10.0 %all-to-all-done = bf16[64,16,128]{2,1,0:T(8,128)(2,1)S(1)} async-done(((bf16[64,16,128]{2,1,0:T(8,128)(2,1)}), bf16[64,16,128]{2,1,0:T(8,128)(2,1)S(1)}, u32[]{:S(2)}, u32[]{:S(2)}) %all-to-all-start) | async-done | bytes 262176 | tf_op jit(solution)/shard_map/all_to_all | solution.py:367
  47.5 1.0 %finish.1 = (bf16[512,320]{1,0:T(8,128)(2,1)S(1)}, bf16[256,128]{1,0:T(8,128)(2,1)}) custom-call(bf16[512,320]{1,0:T(8,128)(2,1)S(1)} %copy.53.state_ref, f32[8,512]{1,0:T(8,128)S(1)} %copy-done.5, bf16[320,320]{1,0:T(8,128)(2,1)S(1)} %copy-done.1, bf16[128,320]{1,0:T(8,128)(2,1)S(1)} %copy.54.wall_tile_ref, f32[512,320]{1,0:T(8,128)S(1)} %get-tuple-element.15.rest_ref, ...), custom_call_target="tpu_custom_call" | custom-call | flops 209715200 | bytes 1552384 | tf_op jit(solution)/shard_map/finish/pallas_call | solution.py:274
  48.5 0.9 %copy.55 = bf16[512,320]{0,1:T(8,128)(2,1)} copy(bf16[512,320]{1,0:T(8,128)(2,1)S(1)} %get-tuple-element.24) | data formatting | bytes 655360
  (7 shorter events, 0.1 us)
Async XLA Ops:
  0.6 10.5 %copy-start.12 = (s32[512,6]{0,1:T(8,128)S(1)}, s32[512,6]{0,1:T(8,128)}, u32[]{:S(2)}) copy-start(s32[512,6]{0,1:T(8,128)} %param.25) | copy-start | bytes 36868
  0.6 10.9 %copy-start.9 = (bf16[512,320]{0,1:T(8,128)(2,1)S(1)}, bf16[512,320]{0,1:T(8,128)(2,1)}, u32[]{:S(2)}) copy-start(bf16[512,320]{0,1:T(8,128)(2,1)} %param.16) | copy-start | bytes 983044
  0.7 11.1 %copy-start.10 = (bf16[512,320]{0,1:T(8,128)(2,1)S(1)}, bf16[512,320]{0,1:T(8,128)(2,1)}, u32[]{:S(2)}) copy-start(bf16[512,320]{0,1:T(8,128)(2,1)} %param.17) | copy-start | bytes 983044
  3.9 8.2 %copy-start.5 = (f32[8,512]{1,0:T(8,128)S(1)}, f32[8,512]{1,0:T(8,128)}, u32[]{:S(2)}) copy-start(f32[8,512]{1,0:T(8,128)} %metric_ref.5) | copy-start | bytes 49156
  3.9 8.2 %copy-start.7 = (s32[512]{0:T(512)S(1)}, s32[512]{0:T(512)}, u32[]{:S(2)}) copy-start(s32[512]{0:T(512)} %param.26) | copy-start | bytes 6148
  3.9 8.2 %copy-start.8 = (s32[256]{0:T(256)S(1)}, s32[256]{0:T(256)}, u32[]{:S(2)}) copy-start(s32[256]{0:T(256)} %param.27) | copy-start | bytes 3076
  4.3 12.6 %collective-permute-start = (bf16[64,768]{1,0:T(8,128)(2,1)S(1)}, bf16[64,768]{1,0:T(8,128)(2,1)S(1)}, u32[]{:S(2)}, u32[]{:S(2)}) collective-permute-start(bf16[64,768]{1,0:T(8,128)(2,1)S(1)} %get-tuple-element.36), channel_id=1, source_target_pairs={{0,1},{1,2},{2,3},{3,4},{4,5},{5,6},{6,7},{7,8},{8,9},{9,10},{10,1... | collective-permute-start | bytes 294920 | tf_op jit(solution)/shard_map/ppermute | solution.py:321
  9.2 7.7 %collective-permute-start.1 = (bf16[64,768]{1,0:T(8,128)(2,1)S(1)}, bf16[64,768]{1,0:T(8,128)(2,1)S(1)}, u32[]{:S(2)}, u32[]{:S(2)}) collective-permute-start(bf16[64,768]{1,0:T(8,128)(2,1)S(1)} %get-tuple-element.35), channel_id=1, source_target_pairs={{1,0},{2,1},{3,2},{4,3},{5,4},{6,5},{7,6},{8,7},{9,8},{10,9},{11,1... | collective-permute-start | bytes 294920 | tf_op jit(solution)/shard_map/ppermute | solution.py:322
  12.0 1.5 %copy-start.6 = (bf16[8,320,320]{2,1,0:T(8,128)(2,1)S(1)}, bf16[8,320,320]{2,1,0:T(8,128)(2,1)}, u32[]{:S(2)}) copy-start(bf16[8,320,320]{2,1,0:T(8,128)(2,1)} %basis_ref.1) | copy-start | bytes 4915204
  13.6 3.3 %copy-start = (bf16[6,320,320]{2,1,0:T(8,128)(2,1)S(1)}, bf16[6,320,320]{2,1,0:T(8,128)(2,1)}, u32[]{:S(2)}) copy-start(bf16[6,320,320]{2,1,0:T(8,128)(2,1)} %faces_ref.1) | copy-start | bytes 3686404
  13.6 3.4 %copy-start.1 = (bf16[320,320]{1,0:T(8,128)(2,1)S(1)}, bf16[320,320]{1,0:T(8,128)(2,1)}, u32[]{:S(2)}) copy-start(bf16[320,320]{1,0:T(8,128)(2,1)} %precond_ref.3) | copy-start | bytes 614404
  13.6 3.4 %copy-start.3 = (bf16[320,128]{1,0:T(8,128)(2,1)S(1)}, bf16[320,128]{1,0:T(8,128)(2,1)}, u32[]{:S(2)}) copy-start(bf16[320,128]{1,0:T(8,128)(2,1)} %traction_tile_ref.1) | copy-start | bytes 245764
  13.6 3.4 %copy-start.4 = (bf16[256,128]{1,0:T(8,128)(2,1)S(1)}, bf16[256,128]{1,0:T(8,128)(2,1)}, u32[]{:S(2)}) copy-start(bf16[256,128]{1,0:T(8,128)(2,1)} %mode_ref.1) | copy-start | bytes 196612
  17.0 18.5 %copy-start.11 = (bf16[128,320]{0,1:T(8,128)(2,1)S(1)}, bf16[128,320]{0,1:T(8,128)(2,1)}, u32[]{:S(2)}) copy-start(bf16[128,320]{0,1:T(8,128)(2,1)} %param.22) | copy-start | bytes 245764
  21.8 0.7 %copy-start.2 = (bf16[512,320]{1,0:T(8,128)(2,1)}, bf16[512,320]{1,0:T(8,128)(2,1)S(1)}, u32[]{:S(2)}) copy-start(bf16[512,320]{1,0:T(8,128)(2,1)S(1)} %get-tuple-element.25) | copy-start | bytes 983044
  22.6 24.9 %all-to-all-start = ((bf16[64,16,128]{2,1,0:T(8,128)(2,1)}), bf16[64,16,128]{2,1,0:T(8,128)(2,1)S(1)}, u32[]{:S(2)}, u32[]{:S(2)}) async-start(bf16[64,16,128]{2,1,0:T(8,128)(2,1)} %bitcast.2), calls=%async_computation | async-start | bytes 524288 | tf_op jit(solution)/shard_map/all_to_all | solution.py:367

commit v2 on v0

v2 whole, which is shorter than its diff:
```python
import jax
import jax.numpy as jnp
from jax import lax
from jax.experimental import pallas as pl
from jax.experimental.pallas import tpu as pltpu
from jax.sharding import PartitionSpec as P

HALO = 64
LANES = 128
MAIN = 256
CAP = 8
NOWHERE = -1000.0
F32 = jnp.float32
BF16 = jnp.bfloat16
NT = (((1,), (1,)), ((), ()))


def mm(left, right):
    return jnp.dot(left, right, preferred_element_type=F32)


def mm_nt(left, right):
    return lax.dot_general(left, right, NT, preferred_element_type=F32)


def lane(rows, width=LANES):
    return lax.broadcasted_iota(jnp.int32, (rows, width), 1)


def hot(left, right):
    return jnp.where(left == right, 1.0, 0.0).astype(BF16)


def half_roll(x):
    return jnp.concatenate([x[:, HALO:], x[:, :HALO]], axis=1)


def columns_of(rows):
    fill = jnp.zeros((LANES - rows.shape[0], rows.shape[1]), F32)
    return jnp.transpose(jnp.concatenate([rows, fill], axis=0))


def transposed(x):
    m, n = x.shape
    x = x.astype(F32)
    if m % LANES:
        x = jnp.concatenate([x, jnp.zeros((LANES - m % LANES, n), F32)], axis=0)
    if n % LANES:
        x = jnp.concatenate([x, jnp.zeros((x.shape[0], LANES - n % LANES), F32)], axis=1)
    return jnp.transpose(x)[:n, :m]


def offsets(neighbors, first, elems):
    position = first + lax.broadcasted_iota(jnp.int32, neighbors.shape, 1)
    distance = ((neighbors - position + HALO) & (elems - 1)) - HALO
    return distance, neighbors >= 0, position


def padded_rows(x, rows):
    return jnp.concatenate([x, jnp.zeros((rows - x.shape[0], x.shape[1]), x.dtype)], axis=0)


def key_column(key_row):
    return jnp.transpose(jnp.broadcast_to(key_row, (LANES, key_row.shape[1])))[:, :1]


def rank_row(key_row, base_row):
    column = key_column(key_row)
    return jnp.sum(jnp.where((column < key_row) & (column >= base_row), 1.0, 0.0), axis=0, keepdims=True)


def rank_column(key_row, base_row):
    key, base = key_column(key_row), key_column(base_row)
    return jnp.sum(jnp.where((key_row < key) & (key_row >= base), 1.0, 0.0), axis=1, keepdims=True)


def node_keys(target, elems):
    nodes = target.shape[1]
    device = (target // elems).astype(F32)
    key = device * nodes + lax.broadcasted_iota(jnp.int32, (1, nodes), 1).astype(F32)
    return device, key, device * nodes


def adjoint_halo(parity, same_chip, next_chip):
    mask = (lane(same_chip.shape[0]) < HALO).astype(jnp.int32) != parity
    return jnp.where(mask, next_chip.astype(F32), same_chip.astype(F32))


def state_halo(parity, same_chip, next_chip):
    mask = (lane(same_chip.shape[0]) < HALO).astype(jnp.int32) != parity
    return jnp.where(mask, same_chip.astype(F32), next_chip.astype(F32))


def begin(copies, sems):
    started = [pltpu.make_async_copy(a, b, sems.at[i]) for i, (a, b) in enumerate(copies)]
    for copy in started:
        copy.start()
    return started


def pack_kernel(
    parity_ref,
    state_hbm,
    adjoint_hbm,
    neighbors_hbm,
    same_chip_ref,
    next_chip_ref,
    adjoint_ref,
    neighbors_ref,
    first_ref,
    last_ref,
    sems,
):
    width, elems = adjoint_ref.shape
    final = elems - LANES
    copies = begin(
        [
            (neighbors_hbm, neighbors_ref),
            (state_hbm.at[:, :LANES], first_ref),
            (state_hbm.at[:, final:], last_ref),
            (adjoint_hbm, adjoint_ref),
        ],
        sems,
    )
    low = lane(width) < HALO
    rows = same_chip_ref.shape[0] - width
    copies[0].wait()

    def codes(first):
        distance, linked, _ = offsets(neighbors_ref[:, first : first + LANES], first, elems)
        code = jnp.where(linked, distance + (HALO + 1), 0).astype(F32)
        return half_roll(padded_rows(code, rows)).astype(BF16)

    up_code, down_code = codes(final), codes(0)
    for copy in copies[1:]:
        copy.wait()

    def adjoint(first):
        return half_roll(adjoint_ref[:, first : first + LANES].astype(F32))

    up = jnp.where(low, adjoint(final), last_ref[...].astype(F32)).astype(BF16)
    down = jnp.where(low, first_ref[...].astype(F32), adjoint(0)).astype(BF16)

    @pl.when(parity_ref[0] == 0)
    def _():
        same_chip_ref[:width, :], same_chip_ref[width:, :] = up, up_code
        next_chip_ref[:width, :], next_chip_ref[width:, :] = down, down_code

    @pl.when(parity_ref[0] != 0)
    def _():
        same_chip_ref[:width, :], same_chip_ref[width:, :] = down, down_code
        next_chip_ref[:width, :], next_chip_ref[width:, :] = up, up_code


def spread(x_ref, first, count, lanes, gathered):
    for f in range(count):
        one = gathered[:, f * LANES : (f + 1) * LANES].astype(BF16)
        rest = one.shape[0] - MAIN
        x_ref[first + f * MAIN : first + (f + 1) * MAIN, lanes] = one[:MAIN, :]
        start = first + count * MAIN + f * rest
        x_ref[start : start + rest, lanes] = one[MAIN:, :]


def side_by_side(w_ref, tiles_ref):
    count, width, _ = tiles_ref.shape
    for k in range(count):
        w_ref[:, k * MAIN : (k + 1) * MAIN] = tiles_ref[k, :, :MAIN]
    w_ref[:, count * MAIN :] = jnp.concatenate(
        [tiles_ref[k, :, MAIN:] for k in range(count)], axis=1
    )


def inner_kernel(
    adjoint_ref,
    neighbors_ref,
    source_hbm,
    metric_hbm,
    basis_hbm,
    faces_hbm,
    precond_hbm,
    traction_tile_hbm,
    mode_hbm,
    wall_node_hbm,
    wall_target_hbm,
    partial_ref,
    inner_ref,
    w_faces_ref,
    traction_t_ref,
    srow_ref,
    out_modes_ref,
    out_traction_ref,
    metric_ref,
    basis_ref,
    faces_ref,
    precond_ref,
    x_ref,
    w_ref,
    source_ref,
    traction_tile_ref,
    mode_ref,
    wall_node_ref,
    wall_target_ref,
    sems,
):
    width, elems = adjoint_ref.shape
    geo, count = basis_ref.shape[0], faces_ref.shape[0]
    tail = width - MAIN
    nodes = mode_ref.shape[0]
    copies = begin(
        [
            (metric_hbm, metric_ref),
            (wall_node_hbm, wall_node_ref),
            (wall_target_hbm, wall_target_ref),
            (faces_hbm, faces_ref),
            (basis_hbm, basis_ref),
            (mode_hbm, mode_ref),
            (source_hbm, source_ref),
            (precond_hbm, precond_ref),
            (traction_tile_hbm, traction_tile_ref),
        ],
        sems,
    )
    metric_copy, node_copy, target_copy, faces_copy, basis_copy, mode_copy = copies[:6]

    distance, linked, position = offsets(neighbors_ref[...], 0, elems)
    target = jnp.where(linked, (position + distance).astype(F32), NOWHERE)
    span = LANES + 2 * HALO
    base = geo * width
    for b in range(elems // LANES):
        start = min(max(b * LANES - HALO, 0), elems - span)
        row = b * LANES + lax.broadcasted_iota(jnp.int32, (LANES, span), 0)
        named = jnp.concatenate(
            [hot(row.astype(F32), target[f : f + 1, start : start + span]) for f in range(count)],
            axis=0,
        )
        gathered = mm_nt(adjoint_ref[:, start : start + span], named)
        spread(x_ref, base, count, slice(b * LANES, (b + 1) * LANES), gathered)

    metric_copy.wait()
    value = adjoint_ref[...].astype(F32)
    for k in range(geo):
        scaled = (value * metric_ref[k : k + 1, :]).astype(BF16)
        x_ref[k * MAIN : (k + 1) * MAIN, :] = scaled[:MAIN, :]
        start = geo * MAIN + k * tail
        x_ref[start : start + tail, :] = scaled[MAIN:, :]

    node_copy.wait()
    target_copy.wait()
    node = wall_node_ref[...]
    on_wall = node >= 0
    owner = jnp.where(on_wall, node // nodes, 0).astype(F32)
    elem_slot = owner * CAP + rank_row(node.astype(F32), owner * nodes)
    elem_slot = jnp.where(on_wall, elem_slot, NOWHERE)
    device, key, key_base = node_keys(wall_target_ref[...], elems)
    node_slot = device * CAP + rank_row(key, key_base)
    srow_ref[...] = jnp.zeros(srow_ref.shape, F32)
    srow_ref[0:1, :] = elem_slot
    srow_ref[1:2, :nodes] = node_slot

    faces_copy.wait()
    side_by_side(w_faces_ref, faces_ref)
    total = mm(w_faces_ref[...], x_ref[base:, :])
    basis_copy.wait()
    side_by_side(w_ref, basis_ref)
    total += mm(w_ref[...], x_ref[:base, :])
    for copy in copies[5:]:
        copy.wait()
    rest = source_ref[...].astype(F32) - total
    last = elems - LANES
    partial_ref[:, :LANES] = rest[:, :LANES]
    partial_ref[:, LANES:] = rest[:, last:]

    update = mm(precond_ref[...], rest[:, LANES:last].astype(BF16))
    inverse = 1.0 / metric_ref[0:1, LANES:last]
    inner = (value[:, LANES:last] + update * inverse).astype(BF16)
    inner_ref[...] = inner
    traction_t = transposed(traction_tile_ref[...]).astype(BF16)
    traction_t_ref[...] = traction_t
    traction = mm(traction_t, inner).astype(BF16)

    slots = out_modes_ref.shape[0]
    place = lax.broadcasted_iota(jnp.int32, (slots, nodes), 0).astype(F32)
    out_modes_ref[...] = mm(hot(place, node_slot), mode_ref[...])
    place = lax.broadcasted_iota(jnp.int32, (slots, last - LANES), 0).astype(F32)
    out_traction_ref[...] = mm_nt(hot(place, elem_slot[:, LANES:last]), traction)


def edge_kernel(
    parity_ref,
    same_chip_ref,
    next_chip_ref,
    adjoint_ref,
    metric_ref,
    partial_ref,
    inner_ref,
    w_faces_ref,
    precond_ref,
    traction_t_ref,
    srow_ref,
    out_modes_ref,
    out_traction_ref,
    new_adjoint_ref,
    send_ref,
    x_ref,
):
    width, elems = adjoint_ref.shape
    count = w_faces_ref.shape[1] // width
    last = elems - LANES
    message = adjoint_halo(parity_ref[0], same_chip_ref[...], next_chip_ref[...])
    halo, code = message[:width, :].astype(BF16), message[width : width + 8, :]
    position = lane(8)
    shift = jnp.where(position < HALO, -(2 * HALO + 1), -1)
    target = jnp.where(code == 0.0, NOWHERE, code + (position + shift).astype(F32))
    row = lax.broadcasted_iota(jnp.int32, (LANES, LANES), 0).astype(F32)
    named = jnp.concatenate([hot(row, target[f : f + 1, :]) for f in range(count)], axis=0)
    spread(x_ref, 0, count, slice(0, LANES), mm_nt(halo, named))
    owed = mm(w_faces_ref[...], x_ref[...])
    low = lane(width) < HALO
    rest = jnp.concatenate(
        [
            partial_ref[:, :LANES] - jnp.where(low, owed, 0.0),
            partial_ref[:, LANES:] - jnp.where(low, 0.0, owed),
        ],
        axis=1,
    )
    update = mm(precond_ref[...], rest.astype(BF16))

    def ends(x):
        return jnp.concatenate([x[:, :LANES], x[:, last:]], axis=1)

    inverse = 1.0 / ends(metric_ref[0:1, :])
    edge = (ends(adjoint_ref[...]).astype(F32) + update * inverse).astype(BF16)
    new_adjoint_ref[:, :LANES] = edge[:, :LANES]
    new_adjoint_ref[:, LANES:last] = inner_ref[...]
    new_adjoint_ref[:, last:] = edge[:, LANES:]
    traction = mm(traction_t_ref[...], edge).astype(BF16)
    slots, lanes = out_modes_ref.shape
    place = lax.broadcasted_iota(jnp.int32, (slots, 2 * LANES), 0).astype(F32)
    out_traction = out_traction_ref[...] + mm_nt(hot(place, ends(srow_ref[0:1, :])), traction)
    both = [x.reshape(slots // CAP, CAP, lanes) for x in (out_modes_ref[...], out_traction)]
    send_ref[...] = jnp.concatenate(both, axis=1).reshape(2 * slots, lanes).astype(BF16)


def forward_kernel(
    parity_ref,
    same_chip_ref,
    next_chip_ref,
    metric_ref,
    precond_ref,
    neighbors_ref,
    srow_ref,
    basis_ref,
    faces_ref,
    state_hbm,
    right_hbm,
    wall_tile_t_hbm,
    wall_target_hbm,
    after_hbm,
    most_ref,
    wall_map_ref,
    elem_hot_ref,
    node_hot_ref,
    x_ref,
    w_ref,
    state_ref,
    right_ref,
    wall_tile_t_ref,
    wall_target_ref,
    sems,
):
    width, elems = state_ref.shape
    copies = begin(
        [
            (state_hbm, state_ref),
            (right_hbm, right_ref),
            (wall_tile_t_hbm, wall_tile_t_ref),
            (wall_target_hbm, wall_target_ref),
        ],
        sems,
    )
    copies[0].wait()
    geo, count = basis_ref.shape[0], faces_ref.shape[0]
    tail = width - MAIN
    base = geo * width
    factors = columns_of(metric_ref[...])
    value = transposed(state_ref[...])
    tails = []
    for k in range(geo):
        scaled = (value * factors[:, k : k + 1]).astype(BF16)
        x_ref[:, k * MAIN : (k + 1) * MAIN] = scaled[:, :MAIN]
        tails.append(scaled[:, MAIN:])
    x_ref[:, geo * MAIN : base] = jnp.concatenate(tails, axis=1)

    distance, linked, position = offsets(neighbors_ref[...], 0, elems)
    source = position + distance
    span = LANES + 2 * HALO
    last = elems - LANES
    block = position // LANES
    shift = jnp.where(
        position < LANES,
        jnp.where(source < 0, span, 0),
        jnp.where(
            position >= last,
            jnp.where(source >= elems, -elems, span - elems),
            HALO - block * LANES,
        ),
    )
    column = columns_of(padded_rows(jnp.where(linked, (source + shift).astype(F32), NOWHERE), 8))
    halo = state_halo(parity_ref[0], same_chip_ref[...], next_chip_ref[...])[:width, :].astype(BF16)
    place = lane(LANES, span).astype(F32)
    for b in range(elems // LANES):
        if b == 0:
            beside = jnp.concatenate([state_ref[:, : span - HALO], halo[:, HALO:]], axis=1)
        elif b == elems // LANES - 1:
            beside = jnp.concatenate([halo[:, :HALO], state_ref[:, elems - span + HALO :]], axis=1)
        else:
            beside = state_ref[:, b * LANES - HALO : b * LANES - HALO + span]
        rows = slice(b * LANES, (b + 1) * LANES)
        named = jnp.concatenate([hot(place, column[rows, f : f + 1]) for f in range(count)], axis=0)
        gathered = mm_nt(named, beside).astype(BF16)
        tails = []
        for f in range(count):
            one = gathered[f * LANES : (f + 1) * LANES, :]
            x_ref[rows, base + f * MAIN : base + (f + 1) * MAIN] = one[:, :MAIN]
            tails.append(one[:, MAIN:])
        x_ref[rows, base + count * MAIN :] = jnp.concatenate(tails, axis=1)

    for copy in copies[1:]:
        copy.wait()
    for first, tiles_ref in ((0, basis_ref), (base, faces_ref)):
        number = tiles_ref.shape[0]
        for k in range(number):
            w_ref[first + k * MAIN : first + (k + 1) * MAIN, :] = tiles_ref[k, :MAIN, :]
            start = first + number * MAIN + k * tail
            w_ref[start : start + tail, :] = tiles_ref[k, MAIN:, :]
    applied = mm(x_ref[...], w_ref[...])
    rest = (right_ref[...].astype(F32) - transposed(applied)).astype(BF16)

    precond_t = transposed(precond_ref[...]).astype(BF16)
    inverse = 1.0 / metric_ref[0:1, :]
    most_ref[...] = state_ref[...].astype(F32) + mm(precond_t, rest) * inverse
    wall_map_ref[...] = mm(precond_t, wall_tile_t_ref[...]).astype(BF16)
    slots = elem_hot_ref.shape[0]
    nodes = node_hot_ref.shape[0]
    place = lax.broadcasted_iota(jnp.int32, (slots, elems), 0).astype(F32)
    elem_hot_ref[...] = hot(place, srow_ref[0:1, :])
    device, key, key_base = node_keys(wall_target_ref[...], elems)
    node_slot = key_column(device) * CAP + rank_column(key, key_base)
    node_hot_ref[...] = hot(lane(nodes, slots).astype(F32), node_slot)


def finish_kernel(
    metric_ref,
    most_ref,
    wall_map_ref,
    elem_hot_ref,
    node_hot_ref,
    received_ref,
    new_state_hbm,
    wall_load_hbm,
    new_state_ref,
    wall_load_ref,
    sems,
):
    slots, lanes = elem_hot_ref.shape[0], received_ref.shape[1]
    elems = most_ref.shape[1]
    received = received_ref[...].astype(F32).reshape(slots // CAP, 2 * CAP, lanes)
    modes_t = jnp.transpose(received[:, :CAP, :].reshape(slots, lanes)).astype(BF16)
    traction = received[:, CAP:, :].reshape(slots, lanes).astype(BF16)
    inverse = 1.0 / metric_ref[0:1, :]
    copies = []
    step = 2 * LANES
    for first in range(0, elems, step):
        part = slice(first, first + step)
        wall_modes_t = mm(modes_t, elem_hot_ref[:, part]).astype(BF16)
        update = mm(wall_map_ref[...], wall_modes_t)
        new_state_ref[:, part] = (most_ref[:, part] + update * inverse[:, part]).astype(BF16)
        pair = (new_state_ref.at[:, part], new_state_hbm.at[:, part])
        copies += begin([pair], sems.at[first // step : first // step + 1])
    wall_load_ref[...] = mm(node_hot_ref[...], traction).astype(BF16)
    count = len(copies)
    copies += begin([(wall_load_ref, wall_load_hbm)], sems.at[count : count + 1])
    for copy in copies:
        copy.wait()


NEAR = pl.BlockSpec(memory_space=pltpu.VMEM)
FAR = pl.BlockSpec(memory_space=pltpu.HBM)
SCALAR = pl.BlockSpec(memory_space=pltpu.SMEM)


def call(kernel, name, outs, scratch, args, flops, specs, out_space=pltpu.VMEM, copies=0):
    size = sum(a.size * a.dtype.itemsize for a in args)
    sems = [pltpu.SemaphoreType.DMA((copies,))] if copies else []
    spec_of = {"s": SCALAR, "n": NEAR, "f": FAR}
    space_of = {"n": pltpu.VMEM, "f": pltpu.HBM}
    args = [
        pltpu.with_memory_space_constraint(a, space_of[c]) if c in space_of else a
        for a, c in zip(args, specs, strict=True)
    ]
    return pl.pallas_call(
        kernel,
        out_shape=[out_space(shape, dtype) for shape, dtype in outs],
        in_specs=[spec_of[c] for c in specs],
        out_specs=[pl.BlockSpec(memory_space=out_space)] * len(outs),
        scratch_shapes=[pltpu.VMEM(shape, dtype) for shape, dtype in scratch] + sems,
        compiler_params=pltpu.CompilerParams(vmem_limit_bytes=28 * 1024 * 1024),
        cost_estimate=pl.CostEstimate(flops=flops, bytes_accessed=size, transcendentals=0),
        name=name,
    )(*args)


def on_device(
    state,
    adjoint,
    right_side,
    source,
    metric,
    basis_tiles,
    face_tiles,
    precond,
    wall_tile,
    traction_tile,
    mode_rows,
    neighbors,
    wall_node,
    wall_target,
):
    elems, width = state.shape
    nodes, lanes = mode_rows.shape
    geo, faces = basis_tiles.shape[0], face_tiles.shape[0]
    devices = lax.axis_size("elem")
    slots = devices * CAP
    state, adjoint, right_side, source = state.T, adjoint.T, right_side.T, source.T
    neighbors = neighbors.T
    wall_node, wall_target = wall_node.reshape(1, elems), wall_target.reshape(1, nodes)
    parity = (lax.axis_index("elem") % 2).reshape(1)
    unit = 2 * elems * width * width

    def like(x):
        return (x.shape, x.dtype)

    message = ((width + 16, LANES), BF16)
    same_chip, next_chip, adjoint, neighbors = call(
        pack_kernel,
        "pack",
        [message, message, like(adjoint), like(neighbors)],
        [((width, LANES), BF16), ((width, LANES), BF16)],
        (parity, state, adjoint, neighbors),
        1000,
        "sfff",
        copies=4,
    )
    pairs = [(i, i + 1) for i in range(1, devices - 1, 2)]
    next_chip = lax.ppermute(next_chip, "elem", pairs + [(j, i) for i, j in pairs])
    pairs = [(i, i + 1) for i in range(0, devices, 2)]
    same_chip = lax.ppermute(same_chip, "elem", pairs + [(j, i) for i, j in pairs])

    (
        partial,
        inner,
        w_faces,
        traction_t,
        srow,
        out_modes,
        out_traction,
        metric,
        basis_tiles,
        face_tiles,
        precond,
    ) = call(
        inner_kernel,
        "inner",
        [
            ((width, 2 * LANES), F32),
            ((width, elems - 2 * LANES), BF16),
            ((width, faces * width), BF16),
            ((lanes, width), BF16),
            ((8, elems), F32),
            ((slots, lanes), F32),
            ((slots, lanes), F32),
            like(metric),
            like(basis_tiles),
            like(face_tiles),
            like(precond),
        ],
        [
            (((geo + faces) * width, elems), BF16),
            ((width, geo * width), BF16),
            like(source),
            like(traction_tile),
            like(mode_rows),
            like(wall_node),
            like(wall_target),
        ],
        (
            adjoint,
            neighbors,
            source,
            metric,
            basis_tiles,
            face_tiles,
            precond,
            traction_tile,
            mode_rows,
            wall_node,
            wall_target,
        ),
        (geo + faces + 3) * unit,
        "nnfffffffff",
        copies=9,
    )
    new_adjoint, send = call(
        edge_kernel,
        "edge",
        [((width, elems), BF16), ((2 * slots, lanes), BF16)],
        [((faces * width, LANES), BF16)],
        (
            parity,
            same_chip,
            next_chip,
            adjoint,
            metric,
            partial,
            inner,
            w_faces,
            precond,
            traction_t,
            srow,
            out_modes,
            out_traction,
        ),
        3 * unit,
        "snnnnnnnnnnnn",
    )
    received = lax.all_to_all(send, "elem", 0, 0, tiled=True)
    most, wall_map, elem_hot, node_hot = call(
        forward_kernel,
        "forward",
        [
            ((width, elems), F32),
            ((width, lanes), BF16),
            ((slots, elems), BF16),
            ((nodes, slots), BF16),
        ],
        [
            ((elems, (geo + faces) * width), BF16),
            (((geo + faces) * width, width), BF16),
            like(state),
            like(right_side),
            like(wall_tile.T),
            like(wall_target),
        ],
        (
            parity,
            same_chip,
            next_chip,
            metric,
            precond,
            neighbors,
            srow,
            basis_tiles,
            face_tiles,
            state,
            right_side,
            wall_tile.T,
            wall_target,
            new_adjoint,
        ),
        (geo + faces + 3) * unit,
        "snnnnnnnnffffn",
        copies=4,
    )
    new_state, wall_load = call(
        finish_kernel,
        "finish",
        [((width, elems), BF16), ((nodes, lanes), BF16)],
        [((width, elems), BF16), ((nodes, lanes), BF16)],
        (metric, most, wall_map, elem_hot, node_hot, received),
        2 * unit,
        "nnnnnn",
        out_space=pltpu.HBM,
        copies=elems // (2 * LANES) + 1,
    )
    return (new_state.T, new_adjoint.T, wall_load)


def solution(mesh):
    rows = P(("phase", "elem"), None)
    return jax.shard_map(
        on_device,
        mesh=mesh,
        in_specs=(
            rows,
            rows,
            rows,
            rows,
            P(None, "elem"),
            P("phase", None, None),
            P("phase", None, None),
            P("phase", None),
            P("phase", None),
            P("phase", None),
            rows,
            P("elem", None),
            P("elem"),
            P("elem"),
        ),
        out_specs=(rows, rows, rows),
        check_vma=False,
    )
```

time: 191 us -> 39.6 us (0.21)
  waiting for transfers between devices: 65.9 us -> 1.33 us
  local copies, waits for them, and re-layouts: 43.3 us -> 4.93 us
  matrix products: 26.6 us -> 0 us
  other arithmetic: 26.6 us -> 0 us
  Pallas kernels: 0 us -> 16.6 us
  between operations: 15 us -> 0.7 us
  starting transfers between devices: 12.8 us -> 15.7 us
    all_gather x2 -> x0, waiting for transfers between devices: 65 us -> none  [the longest x1 65 us: on_device(): gathered_load = lax.all_gather(traction, 'elem', axis=0, tiled=True)]
    dot_general x30 -> x0, matrix products: 26.6 us -> none  [the longest x14 13.6 us: times_transposed(): lax.dot_general(left, right, (((1,), (1,)), ((), ())), preferred_element_...]
    gather x8 -> x0, local copies, waits for them, and re-layouts: 25 us -> none  [the longest x6 15.4 us: on_device(): extended[local_index[:, face]]]
    scatter-add x6 -> x0, other arithmetic: 24.4 us -> none  [on_device(): collected = collected.at[local_index[:, face]].add(pushed)]
    pallas_call x0 -> x5, Pallas kernels: none -> 16.6 us  [call(): pl.pallas_call(kernel, out_shape=[out_space(shape, dtype) for shape, dtyp...]
    mul x6 -> x0, local copies, waits for them, and re-layouts: 11.6 us -> none  [on_device(): times_transposed(adjoint, face_tiles[face])]
    all_to_all x0 -> x1, starting transfers between devices: none -> 10.5 us  [on_device(): received = lax.all_to_all(send, 'elem', 0, 0, tiled=True)]
    ppermute x4 -> x2, starting transfers between devices: 12.7 us -> 5.24 us  [the longest x1 3.33 us: on_device(): lax.ppermute(same_chip, 'elem', pairs + [(j, i) for i, j in pairs])]
  transfers between devices with their start and end apart: 6 -> 3, of which waited for: 2 -> 1; matrix products, arithmetic and copies ran while one was open for 48% -> 2% of each run, Pallas kernels for 0% -> 30%
where the time goes in v2:
time: 39.6 us; the launch traced here: 39.3 us
  Pallas kernels  16.6 us (42%)
  starting transfers between devices  15.7 us (40%)
  local copies, waits for them, and re-layouts  4.93 us (12%)
  waiting for transfers between devices  1.33 us (3%)
  between operations  0.7 us (2%)
    pallas_call x5, Pallas kernels, call(): pl.pallas_call(kernel, out_shape=[out_space(shape, dtype) for shape, dtyp...  16.6 us
    all_to_all x1, starting transfers between devices, on_device(): received = lax.all_to_all(send, 'elem', 0, 0, tiled=True)  10.5 us
    unnamed x9, local copies, waits for them, and re-layouts  4.93 us
    ppermute x1, starting transfers between devices, on_device(): lax.ppermute(same_chip, 'elem', pairs + [(j, i) for i, j in pairs])  3.33 us
    ppermute x1, starting transfers between devices, on_device(): lax.ppermute(next_chip, 'elem', pairs + [(j, i) for i, j in pairs])  1.91 us
    all_to_all x1, waiting for transfers between devices, on_device(): received = lax.all_to_all(send, 'elem', 0, 0, tiled=True)  1.33 us
  transfers between devices with their start and end apart: 3, of which 1 were waited for; matrix products, arithmetic and copies ran while one was open for 2% of the time, Pallas kernels for 30%

profile of v2, /device:TPU:1, one launch (start us, length us, event | category | flops | bytes accessed | tf_op | source)
XLA Modules:
  0.0 39.3 jit_solution(16507913711904494436)
XLA Ops:
  0.6 1.2 %pack.1 = (bf16[336,128]{1,0:T(8,128)(2,1)S(1)}, bf16[336,128]{1,0:T(8,128)(2,1)S(1)}, bf16[320,512]{1,0:T(8,128)(2,1)S(1)}, s32[6,512]{1,0:T(8,128)S(1)}) custom-call(s32[1]{0:T(128)} %bitcast.parity_ref, bf16[320,512]{1,0:T(8,128)(2,1)} %bitcast.16, bf16[320,512]{1,0:T(8,128)(2,1)} %bitcast.15, s32[6,512]{1,0:T(8,128)} %bitcast.18), custom_call_target="tpu_custom_call" | custom-call | flops 1000 | bytes 667652 | tf_op jit(solution)/shard_map/pack/pallas_call | solution.py:501
  1.9 3.3 %collective-permute-start = (bf16[336,128]{1,0:T(8,128)(2,1)S(1)}, bf16[336,128]{1,0:T(8,128)(2,1)S(1)}, u32[]{:S(2)}, u32[]{:S(2)}) collective-permute-start(bf16[336,128]{1,0:T(8,128)(2,1)S(1)} %get-tuple-element.29), channel_id=1, source_target_pairs={{0,1},{2,3},{4,5},{6,7},{8,9},{10,11},{12,13},{14,15},{16,17},{18,... | collective-permute-start | bytes 258056 | tf_op jit(solution)/shard_map/ppermute | solution.py:557
  5.2 1.9 %collective-permute-start.1 = (bf16[336,128]{1,0:T(8,128)(2,1)S(1)}, bf16[336,128]{1,0:T(8,128)(2,1)S(1)}, u32[]{:S(2)}, u32[]{:S(2)}) collective-permute-start(bf16[336,128]{1,0:T(8,128)(2,1)S(1)} %get-tuple-element.30), channel_id=1, source_target_pairs={{1,2},{3,4},{5,6},{7,8},{9,10},{11,12},{13,14},{15,16},{17,18},{19... | collective-permute-start | bytes 258056 | tf_op jit(solution)/shard_map/ppermute | solution.py:555
  7.1 4.7 %inner.1 = (f32[320,256]{1,0:T(8,128)S(1)}, bf16[320,256]{1,0:T(8,128)(2,1)S(1)}, bf16[320,1920]{1,0:T(8,128)(2,1)S(1)}, bf16[128,320]{1,0:T(8,128)(2,1)S(1)}, f...) custom-call(bf16[320,512]{1,0:T(8,128)(2,1)S(1)} %get-tuple-element., ...), custom_call_target="tpu_custom_call" | custom-call | flops 1782579200 | bytes 3906560 | tf_op jit(solution)/shard_map/inner/pallas_call | solution.py:501
  11.8 0.0 copy-start
  11.8 1.3 %copy-done = bf16[8,320,320]{2,1,0:T(8,128)(2,1)} copy-done((bf16[8,320,320]{2,1,0:T(8,128)(2,1)}, bf16[8,320,320]{2,1,0:T(8,128)(2,1)S(1)}, u32[]{:S(2)}) %copy-start) | copy-done | bytes 1638424
  13.1 0.0 copy-start.2
  13.1 0.0 collective-permute-done.same_chip_ref
  13.1 0.0 collective-permute-done.1.next_chip_ref
  13.1 2.4 %edge.1 = (bf16[320,512]{1,0:T(8,128)(2,1)S(1)}, bf16[1024,128]{1,0:T(8,128)(2,1)}) custom-call(s32[1]{0:T(128)} %bitcast.parity_ref, bf16[336,128]{1,0:T(8,128)(2,1)S(1)} %collective-permute-done.same_chip_ref, bf16[336,128]{1,0:T(8,128)(2,1)S(1)} %collective-permute-done.1.next_chip_ref, bf16[320,512]{1,0:T(8,128)(2,1)S(1)} %get-tuple-element.26.adjoint_ref, ...), custom_call_target="tpu_custom_call" | custom-call | flops 314572800 | bytes 3063812 | tf_op jit(solution)/shard_map/edge/pallas_call | solution.py:501
  15.5 0.0 copy-done.2
  15.5 10.5 %all-to-all-start = ((bf16[64,16,128]{2,1,0:T(8,128)(2,1)}), bf16[64,16,128]{2,1,0:T(8,128)(2,1)S(1)}, u32[]{:S(2)}, u32[]{:S(2)}) async-start(bf16[64,16,128]{2,1,0:T(8,128)(2,1)} %bitcast.9), calls=%async_computation | async-start | bytes 524288 | tf_op jit(solution)/shard_map/all_to_all | solution.py:636
  26.0 0.7 %copy.17 = bf16[512,320]{0,1:T(8,128)(2,1)} copy(bf16[512,320]{0,1:T(8,128)(2,1)S(1)} %bitcast.13) | data formatting | bytes 655360
  26.7 0.0 copy-start.1
  26.7 1.5 %copy-done.1 = bf16[8,320,320]{2,1,0:T(8,128)(2,1)S(1)} copy-done((bf16[8,320,320]{2,1,0:T(8,128)(2,1)S(1)}, bf16[8,320,320]{2,1,0:T(8,128)(2,1)}, u32[]{:S(2)}) %copy-start.1) | copy-done | bytes 1638424
  28.3 0.0 copy-start.3
  28.3 1.4 %copy-done.3 = bf16[6,320,320]{2,1,0:T(8,128)(2,1)S(1)} copy-done((bf16[6,320,320]{2,1,0:T(8,128)(2,1)S(1)}, bf16[6,320,320]{2,1,0:T(8,128)(2,1)}, u32[]{:S(2)}) %copy-start.3) | copy-done | bytes 1228824
  29.7 7.0 %forward.1 = (f32[320,512]{1,0:T(8,128)S(1)}, bf16[320,128]{1,0:T(8,128)(2,1)S(1)}, bf16[512,512]{1,0:T(8,128)(2,1)S(1)}, bf16[256,512]{1,0:T(8,128)(2,1)S(1)}) custom-call(s32[1]{0:T(128)} %bitcast.parity_ref, bf16[336,128]{1,0:T(8,128)(2,1)S(1)} %collective-permute-done.same_chip_ref, bf16[336,128]{1,0:T(8,128)(2,1)S(1)} %collective-permute-done.1.next_chip_ref, ...), custom_call_target="tpu_custom_call" | custom-call | flops 1782579200 | bytes 4355076 | tf_op jit(solution)/shard_map/forward/pallas_call | solution.py:501
  36.7 1.3 %all-to-all-done = bf16[64,16,128]{2,1,0:T(8,128)(2,1)S(1)} async-done(((bf16[64,16,128]{2,1,0:T(8,128)(2,1)}), bf16[64,16,128]{2,1,0:T(8,128)(2,1)S(1)}, u32[]{:S(2)}, u32[]{:S(2)}) %all-to-all-start) | async-done | bytes 262176 | tf_op jit(solution)/shard_map/all_to_all | solution.py:636
  38.0 1.3 %finish.1 = (bf16[320,512]{1,0:T(8,128)(2,1)}, bf16[256,128]{1,0:T(8,128)(2,1)}) custom-call(f32[8,512]{1,0:T(8,128)S(1)} %get-tuple-element.28.metric_ref, f32[320,512]{1,0:T(8,128)S(1)} %get-tuple-element.42.most_ref, bf16[320,128]{1,0:T(8,128)(2,1)S(1)} %get-tuple-element.43.wall_map_ref, bf16[512,512]{1,0:T(8,128)(2,1)S(1)} %get-tuple-element.44.elem_hot_ref, ...), custom_call_target="tpu_custom_call" | custom-call | flops 209715200 | bytes 1802240 | tf_op jit(solution)/shard_map/finish/pallas_call | solution.py:501
Async XLA Ops:
  1.9 11.2 %collective-permute-start = (bf16[336,128]{1,0:T(8,128)(2,1)S(1)}, bf16[336,128]{1,0:T(8,128)(2,1)S(1)}, u32[]{:S(2)}, u32[]{:S(2)}) collective-permute-start(bf16[336,128]{1,0:T(8,128)(2,1)S(1)} %get-tuple-element.29), channel_id=1, source_target_pairs={{0,1},{2,3},{4,5},{6,7},{8,9},{10,11},{12,13},{14,15},{16,17},{18,... | collective-permute-start | bytes 258056 | tf_op jit(solution)/shard_map/ppermute | solution.py:557
  5.2 7.9 %collective-permute-start.1 = (bf16[336,128]{1,0:T(8,128)(2,1)S(1)}, bf16[336,128]{1,0:T(8,128)(2,1)S(1)}, u32[]{:S(2)}, u32[]{:S(2)}) collective-permute-start(bf16[336,128]{1,0:T(8,128)(2,1)S(1)} %get-tuple-element.30), channel_id=1, source_target_pairs={{1,2},{3,4},{5,6},{7,8},{9,10},{11,12},{13,14},{15,16},{17,18},{19... | collective-permute-start | bytes 258056 | tf_op jit(solution)/shard_map/ppermute | solution.py:555
  11.8 1.3 %copy-start = (bf16[8,320,320]{2,1,0:T(8,128)(2,1)}, bf16[8,320,320]{2,1,0:T(8,128)(2,1)S(1)}, u32[]{:S(2)}) copy-start(bf16[8,320,320]{2,1,0:T(8,128)(2,1)S(1)} %get-tuple-element.33.basis_ref) | copy-start | bytes 4915204
  13.1 2.4 %copy-start.2 = (bf16[6,320,320]{2,1,0:T(8,128)(2,1)}, bf16[6,320,320]{2,1,0:T(8,128)(2,1)S(1)}, u32[]{:S(2)}) copy-start(bf16[6,320,320]{2,1,0:T(8,128)(2,1)S(1)} %get-tuple-element.34.faces_ref) | copy-start | bytes 3686404
  15.5 22.5 %all-to-all-start = ((bf16[64,16,128]{2,1,0:T(8,128)(2,1)}), bf16[64,16,128]{2,1,0:T(8,128)(2,1)S(1)}, u32[]{:S(2)}, u32[]{:S(2)}) async-start(bf16[64,16,128]{2,1,0:T(8,128)(2,1)} %bitcast.9), calls=%async_computation | async-start | bytes 524288 | tf_op jit(solution)/shard_map/all_to_all | solution.py:636
  26.7 1.5 %copy-start.1 = (bf16[8,320,320]{2,1,0:T(8,128)(2,1)S(1)}, bf16[8,320,320]{2,1,0:T(8,128)(2,1)}, u32[]{:S(2)}) copy-start(bf16[8,320,320]{2,1,0:T(8,128)(2,1)} %copy-done) | copy-start | bytes 4915204
  28.3 1.4 %copy-start.3 = (bf16[6,320,320]{2,1,0:T(8,128)(2,1)S(1)}, bf16[6,320,320]{2,1,0:T(8,128)(2,1)}, u32[]{:S(2)}) copy-start(bf16[6,320,320]{2,1,0:T(8,128)(2,1)} %copy-done.2) | copy-start | bytes 3686404

commit v3 on v2

--- a/solution.py
+++ b/solution.py
@@ -13,6 +13,7 @@
 F32 = jnp.float32
 BF16 = jnp.bfloat16
 NT = (((1,), (1,)), ((), ()))
+TN = (((0,), (0,)), ((), ()))
 
 
 def mm(left, right):
@@ -21,6 +22,10 @@
 
 def mm_nt(left, right):
     return lax.dot_general(left, right, NT, preferred_element_type=F32)
+
+
+def mm_tn(left, right):
+    return lax.dot_general(left, right, TN, preferred_element_type=F32)
 
 
 def lane(rows, width=LANES):
@@ -161,12 +166,13 @@
         x_ref[start : start + rest, lanes] = one[MAIN:, :]
 
 
-def side_by_side(w_ref, tiles_ref):
-    count, width, _ = tiles_ref.shape
+def side_by_side(w_ref, start, tiles_ref, first, count):
+    width = tiles_ref.shape[1]
     for k in range(count):
-        w_ref[:, k * MAIN : (k + 1) * MAIN] = tiles_ref[k, :, :MAIN]
-    w_ref[:, count * MAIN :] = jnp.concatenate(
-        [tiles_ref[k, :, MAIN:] for k in range(count)], axis=1
+        at = start + k * MAIN
+        w_ref[:, at : at + MAIN] = tiles_ref[first + k, :, :MAIN]
+    w_ref[:, start + count * MAIN : start + count * width] = jnp.concatenate(
+        [tiles_ref[first + k, :, MAIN:] for k in range(count)], axis=1
     )
 
 
@@ -190,11 +196,11 @@
     out_modes_ref,
     out_traction_ref,
     metric_ref,
-    basis_ref,
-    faces_ref,
     precond_ref,
     x_ref,
     w_ref,
+    basis_ref,
+    faces_ref,
     source_ref,
     traction_tile_ref,
     mode_ref,
@@ -206,21 +212,22 @@
     geo, count = basis_ref.shape[0], faces_ref.shape[0]
     tail = width - MAIN
     nodes = mode_ref.shape[0]
+    half = geo // 2
     copies = begin(
         [
             (metric_hbm, metric_ref),
             (wall_node_hbm, wall_node_ref),
             (wall_target_hbm, wall_target_ref),
+            (mode_hbm, mode_ref),
             (faces_hbm, faces_ref),
-            (basis_hbm, basis_ref),
-            (mode_hbm, mode_ref),
+            (basis_hbm.at[:half], basis_ref.at[:half]),
             (source_hbm, source_ref),
             (precond_hbm, precond_ref),
             (traction_tile_hbm, traction_tile_ref),
+            (basis_hbm.at[half:], basis_ref.at[half:]),
         ],
         sems,
     )
-    metric_copy, node_copy, target_copy, faces_copy, basis_copy, mode_copy = copies[:6]
 
     distance, linked, position = offsets(neighbors_ref[...], 0, elems)
     target = jnp.where(linked, (position + distance).astype(F32), NOWHERE)
@@ -236,16 +243,28 @@
         gathered = mm_nt(adjoint_ref[:, start : start + span], named)
         spread(x_ref, base, count, slice(b * LANES, (b + 1) * LANES), gathered)
 
-    metric_copy.wait()
+    for copy in copies[:4]:
+        copy.wait()
     value = adjoint_ref[...].astype(F32)
     for k in range(geo):
         scaled = (value * metric_ref[k : k + 1, :]).astype(BF16)
-        x_ref[k * MAIN : (k + 1) * MAIN, :] = scaled[:MAIN, :]
-        start = geo * MAIN + k * tail
-        x_ref[start : start + tail, :] = scaled[MAIN:, :]
-
-    node_copy.wait()
-    target_copy.wait()
+        start = k // half * half * width
+        main = start + k % half * MAIN
+        x_ref[main : main + MAIN, :] = scaled[:MAIN, :]
+        rest = start + half * MAIN + k % half * tail
+        x_ref[rest : rest + tail, :] = scaled[MAIN:, :]
+
+    copies[4].wait()
+    side_by_side(w_faces_ref, 0, faces_ref, 0, count)
+    total = mm(w_faces_ref[...], x_ref[base:, :])
+    middle = half * width
+    copies[5].wait()
+    side_by_side(w_ref, 0, basis_ref, 0, half)
+    total += mm(w_ref[:, :middle], x_ref[:middle, :])
+    for copy in copies[6:]:
+        copy.wait()
+    side_by_side(w_ref, middle, basis_ref, half, half)
+    total += mm(w_ref[:, middle:], x_ref[middle:base, :])
     node = wall_node_ref[...]
     on_wall = node >= 0
     owner = jnp.where(on_wall, node // nodes, 0).astype(F32)
@@ -256,15 +275,10 @@
     srow_ref[...] = jnp.zeros(srow_ref.shape, F32)
     srow_ref[0:1, :] = elem_slot
     srow_ref[1:2, :nodes] = node_slot
-
-    faces_copy.wait()
-    side_by_side(w_faces_ref, faces_ref)
-    total = mm(w_faces_ref[...], x_ref[base:, :])
-    basis_copy.wait()
-    side_by_side(w_ref, basis_ref)
-    total += mm(w_ref[...], x_ref[:base, :])
-    for copy in copies[5:]:
-        copy.wait()
+    slots = out_modes_ref.shape[0]
+    place = lax.broadcasted_iota(jnp.int32, (slots, nodes), 0).astype(F32)
+    out_modes_ref[...] = mm(hot(place, node_slot), mode_ref[...])
+
     rest = source_ref[...].astype(F32) - total
     last = elems - LANES
     partial_ref[:, :LANES] = rest[:, :LANES]
@@ -278,9 +292,6 @@
     traction_t_ref[...] = traction_t
     traction = mm(traction_t, inner).astype(BF16)
 
-    slots = out_modes_ref.shape[0]
-    place = lax.broadcasted_iota(jnp.int32, (slots, nodes), 0).astype(F32)
-    out_modes_ref[...] = mm(hot(place, node_slot), mode_ref[...])
     place = lax.broadcasted_iota(jnp.int32, (slots, last - LANES), 0).astype(F32)
     out_traction_ref[...] = mm_nt(hot(place, elem_slot[:, LANES:last]), traction)
 
@@ -349,8 +360,8 @@
     precond_ref,
     neighbors_ref,
     srow_ref,
-    basis_ref,
-    faces_ref,
+    basis_hbm,
+    faces_hbm,
     state_hbm,
     right_hbm,
     wall_tile_t_hbm,
@@ -362,6 +373,8 @@
     node_hot_ref,
     x_ref,
     w_ref,
+    basis_ref,
+    faces_ref,
     state_ref,
     right_ref,
     wall_tile_t_ref,
@@ -375,6 +388,8 @@
             (right_hbm, right_ref),
             (wall_tile_t_hbm, wall_tile_t_ref),
             (wall_target_hbm, wall_target_ref),
+            (faces_hbm, faces_ref),
+            (basis_hbm, basis_ref),
         ],
         sems,
     )
@@ -465,14 +480,14 @@
     slots, lanes = elem_hot_ref.shape[0], received_ref.shape[1]
     elems = most_ref.shape[1]
     received = received_ref[...].astype(F32).reshape(slots // CAP, 2 * CAP, lanes)
-    modes_t = jnp.transpose(received[:, :CAP, :].reshape(slots, lanes)).astype(BF16)
+    modes = received[:, :CAP, :].reshape(slots, lanes).astype(BF16)
     traction = received[:, CAP:, :].reshape(slots, lanes).astype(BF16)
     inverse = 1.0 / metric_ref[0:1, :]
     copies = []
     step = 2 * LANES
     for first in range(0, elems, step):
         part = slice(first, first + step)
-        wall_modes_t = mm(modes_t, elem_hot_ref[:, part]).astype(BF16)
+        wall_modes_t = mm_tn(modes, elem_hot_ref[:, part]).astype(BF16)
         update = mm(wall_map_ref[...], wall_modes_t)
         new_state_ref[:, part] = (most_ref[:, part] + update * inverse[:, part]).astype(BF16)
         pair = (new_state_ref.at[:, part], new_state_hbm.at[:, part])
@@ -565,8 +580,6 @@
         out_modes,
         out_traction,
         metric,
-        basis_tiles,
-        face_tiles,
         precond,
     ) = call(
         inner_kernel,
@@ -580,13 +593,13 @@
             ((slots, lanes), F32),
             ((slots, lanes), F32),
             like(metric),
-            like(basis_tiles),
-            like(face_tiles),
             like(precond),
         ],
         [
             (((geo + faces) * width, elems), BF16),
             ((width, geo * width), BF16),
+            like(basis_tiles),
+            like(face_tiles),
             like(source),
             like(traction_tile),
             like(mode_rows),
@@ -608,7 +621,7 @@
         ),
         (geo + faces + 3) * unit,
         "nnfffffffff",
-        copies=9,
+        copies=10,
     )
     new_adjoint, send = call(
         edge_kernel,
@@ -646,6 +659,8 @@
         [
             ((elems, (geo + faces) * width), BF16),
             (((geo + faces) * width, width), BF16),
+            like(basis_tiles),
+            like(face_tiles),
             like(state),
             like(right_side),
             like(wall_tile.T),
@@ -668,8 +683,8 @@
             new_adjoint,
         ),
         (geo + faces + 3) * unit,
-        "snnnnnnnnffffn",
-        copies=4,
+        "snnnnnnffffffn",
+        copies=6,
     )
     new_state, wall_load = call(
         finish_kernel,

time: 39.6 us -> 38 us (0.960)
  local copies, waits for them, and re-layouts: 4.93 us -> 0.73 us
  waiting for transfers between devices: 1.33 us -> 4.3 us
    unnamed x9 -> x1, local copies, waits for them, and re-layouts: 4.93 us -> 0.73 us
    all_to_all x1, waiting for transfers between devices: 1.33 us -> 4.29 us  [on_device(): received = lax.all_to_all(send, 'elem', 0, 0, tiled=True)]
where the time goes in v3:
time: 38 us; the launch traced here: 37.7 us
  Pallas kernels  16.3 us (43%)
  starting transfers between devices  15.7 us (41%)
  waiting for transfers between devices  4.3 us (11%)
  local copies, waits for them, and re-layouts  0.73 us (2%)
  between operations  0.7 us (2%)
    pallas_call x5, Pallas kernels, call(): pl.pallas_call(kernel, out_shape=[out_space(shape, dtype) for shape, dtyp...  16.3 us
    all_to_all x1, starting transfers between devices, on_device(): received = lax.all_to_all(send, 'elem', 0, 0, tiled=True)  10.5 us
    all_to_all x1, waiting for transfers between devices, on_device(): received = lax.all_to_all(send, 'elem', 0, 0, tiled=True)  4.29 us
    ppermute x1, starting transfers between devices, on_device(): lax.ppermute(same_chip, 'elem', pairs + [(j, i) for i, j in pairs])  3.33 us
    ppermute x1, starting transfers between devices, on_device(): lax.ppermute(next_chip, 'elem', pairs + [(j, i) for i, j in pairs])  1.91 us
  transfers between devices with their start and end apart: 3, of which 1 were waited for; matrix products, arithmetic and copies ran while one was open for 2% of the time, Pallas kernels for 30%

profile of v3, /device:TPU:1, one launch (start us, length us, event | category | flops | bytes accessed | tf_op | source)
XLA Modules:
  0.0 37.7 jit_solution(1628289081025874082)
XLA Ops:
  0.6 1.2 %pack.1 = (bf16[336,128]{1,0:T(8,128)(2,1)S(1)}, bf16[336,128]{1,0:T(8,128)(2,1)S(1)}, bf16[320,512]{1,0:T(8,128)(2,1)S(1)}, s32[6,512]{1,0:T(8,128)S(1)}) custom-call(s32[1]{0:T(128)} %bitcast.parity_ref, bf16[320,512]{1,0:T(8,128)(2,1)} %bitcast.16, bf16[320,512]{1,0:T(8,128)(2,1)} %bitcast.15, s32[6,512]{1,0:T(8,128)} %bitcast.18), custom_call_target="tpu_custom_call" | custom-call | flops 1000 | bytes 667652 | tf_op jit(solution)/shard_map/pack/pallas_call | solution.py:516
  1.9 3.3 %collective-permute-start = (bf16[336,128]{1,0:T(8,128)(2,1)S(1)}, bf16[336,128]{1,0:T(8,128)(2,1)S(1)}, u32[]{:S(2)}, u32[]{:S(2)}) collective-permute-start(bf16[336,128]{1,0:T(8,128)(2,1)S(1)} %get-tuple-element.27), channel_id=1, source_target_pairs={{0,1},{2,3},{4,5},{6,7},{8,9},{10,11},{12,13},{14,15},{16,17},{18,... | collective-permute-start | bytes 258056 | tf_op jit(solution)/shard_map/ppermute | solution.py:572
  5.2 1.9 %collective-permute-start.1 = (bf16[336,128]{1,0:T(8,128)(2,1)S(1)}, bf16[336,128]{1,0:T(8,128)(2,1)S(1)}, u32[]{:S(2)}, u32[]{:S(2)}) collective-permute-start(bf16[336,128]{1,0:T(8,128)(2,1)S(1)} %get-tuple-element.28), channel_id=1, source_target_pairs={{1,2},{3,4},{5,6},{7,8},{9,10},{11,12},{13,14},{15,16},{17,18},{19... | collective-permute-start | bytes 258056 | tf_op jit(solution)/shard_map/ppermute | solution.py:570
  7.1 4.4 %inner.1 = (f32[320,256]{1,0:T(8,128)S(1)}, bf16[320,256]{1,0:T(8,128)(2,1)S(1)}, bf16[320,1920]{1,0:T(8,128)(2,1)S(1)}, bf16[128,320]{1,0:T(8,128)(2,1)S(1)}, f...) custom-call(bf16[320,512]{1,0:T(8,128)(2,1)S(1)} %get-tuple-element., ...), custom_call_target="tpu_custom_call" | custom-call | flops 1782579200 | bytes 3906560 | tf_op jit(solution)/shard_map/inner/pallas_call | solution.py:516
  11.6 0.0 collective-permute-done.same_chip_ref
  11.6 0.0 collective-permute-done.1.next_chip_ref
  11.6 2.4 %edge.1 = (bf16[320,512]{1,0:T(8,128)(2,1)S(1)}, bf16[1024,128]{1,0:T(8,128)(2,1)}) custom-call(s32[1]{0:T(128)} %bitcast.parity_ref, bf16[336,128]{1,0:T(8,128)(2,1)S(1)} %collective-permute-done.same_chip_ref, bf16[336,128]{1,0:T(8,128)(2,1)S(1)} %collective-permute-done.1.next_chip_ref, bf16[320,512]{1,0:T(8,128)(2,1)S(1)} %get-tuple-element.24.adjoint_ref, ...), custom_call_target="tpu_custom_call" | custom-call | flops 314572800 | bytes 3063812 | tf_op jit(solution)/shard_map/edge/pallas_call | solution.py:516
  14.0 10.5 %all-to-all-start = ((bf16[64,16,128]{2,1,0:T(8,128)(2,1)}), bf16[64,16,128]{2,1,0:T(8,128)(2,1)S(1)}, u32[]{:S(2)}, u32[]{:S(2)}) async-start(bf16[64,16,128]{2,1,0:T(8,128)(2,1)} %bitcast.9), calls=%async_computation | async-start | bytes 524288 | tf_op jit(solution)/shard_map/all_to_all | solution.py:649
  24.5 0.7 %copy.17 = bf16[512,320]{0,1:T(8,128)(2,1)} copy(bf16[512,320]{0,1:T(8,128)(2,1)S(1)} %bitcast.13) | data formatting | bytes 655360
  25.2 7.0 %forward.1 = (f32[320,512]{1,0:T(8,128)S(1)}, bf16[320,128]{1,0:T(8,128)(2,1)S(1)}, bf16[512,512]{1,0:T(8,128)(2,1)S(1)}, bf16[256,512]{1,0:T(8,128)(2,1)S(1)}) custom-call(s32[1]{0:T(128)} %bitcast.parity_ref, bf16[336,128]{1,0:T(8,128)(2,1)S(1)} %collective-permute-done.same_chip_ref, bf16[336,128]{1,0:T(8,128)(2,1)S(1)} %collective-permute-done.1.next_chip_ref, ...), custom_call_target="tpu_custom_call" | custom-call | flops 1782579200 | bytes 4355076 | tf_op jit(solution)/shard_map/forward/pallas_call | solution.py:516
  32.2 4.3 %all-to-all-done = bf16[64,16,128]{2,1,0:T(8,128)(2,1)S(1)} async-done(((bf16[64,16,128]{2,1,0:T(8,128)(2,1)}), bf16[64,16,128]{2,1,0:T(8,128)(2,1)S(1)}, u32[]{:S(2)}, u32[]{:S(2)}) %all-to-all-start) | async-done | bytes 262176 | tf_op jit(solution)/shard_map/all_to_all | solution.py:649
  36.5 1.2 %finish.1 = (bf16[320,512]{1,0:T(8,128)(2,1)}, bf16[256,128]{1,0:T(8,128)(2,1)}) custom-call(f32[8,512]{1,0:T(8,128)S(1)} %get-tuple-element.26.metric_ref, f32[320,512]{1,0:T(8,128)S(1)} %get-tuple-element.38.most_ref, bf16[320,128]{1,0:T(8,128)(2,1)S(1)} %get-tuple-element.39.wall_map_ref, bf16[512,512]{1,0:T(8,128)(2,1)S(1)} %get-tuple-element.40.elem_hot_ref, ...), custom_call_target="tpu_custom_call" | custom-call | flops 209715200 | bytes 1802240 | tf_op jit(solution)/shard_map/finish/pallas_call | solution.py:516
Async XLA Ops:
  1.9 9.7 %collective-permute-start = (bf16[336,128]{1,0:T(8,128)(2,1)S(1)}, bf16[336,128]{1,0:T(8,128)(2,1)S(1)}, u32[]{:S(2)}, u32[]{:S(2)}) collective-permute-start(bf16[336,128]{1,0:T(8,128)(2,1)S(1)} %get-tuple-element.27), channel_id=1, source_target_pairs={{0,1},{2,3},{4,5},{6,7},{8,9},{10,11},{12,13},{14,15},{16,17},{18,... | collective-permute-start | bytes 258056 | tf_op jit(solution)/shard_map/ppermute | solution.py:572
  5.2 6.3 %collective-permute-start.1 = (bf16[336,128]{1,0:T(8,128)(2,1)S(1)}, bf16[336,128]{1,0:T(8,128)(2,1)S(1)}, u32[]{:S(2)}, u32[]{:S(2)}) collective-permute-start(bf16[336,128]{1,0:T(8,128)(2,1)S(1)} %get-tuple-element.28), channel_id=1, source_target_pairs={{1,2},{3,4},{5,6},{7,8},{9,10},{11,12},{13,14},{15,16},{17,18},{19... | collective-permute-start | bytes 258056 | tf_op jit(solution)/shard_map/ppermute | solution.py:570
  14.0 22.5 %all-to-all-start = ((bf16[64,16,128]{2,1,0:T(8,128)(2,1)}), bf16[64,16,128]{2,1,0:T(8,128)(2,1)S(1)}, u32[]{:S(2)}, u32[]{:S(2)}) async-start(bf16[64,16,128]{2,1,0:T(8,128)(2,1)} %bitcast.9), calls=%async_computation | async-start | bytes 524288 | tf_op jit(solution)/shard_map/all_to_all | solution.py:649

commit v4 on v3

--- a/solution.py
+++ b/solution.py
@@ -103,48 +103,37 @@
     return started
 
 
+def load_kernel(
+    state_hbm, adjoint_hbm, neighbors_hbm, state_ends_ref, adjoint_ends_ref, neighbors_ref, sems
+):
+    last = state_hbm.shape[1] - LANES
+    pairs = [(neighbors_hbm, neighbors_ref)]
+    for far, near in ((state_hbm, state_ends_ref), (adjoint_hbm, adjoint_ends_ref)):
+        pairs.append((far.at[:, :LANES], near.at[:, :LANES]))
+        pairs.append((far.at[:, last:], near.at[:, LANES:]))
+    for copy in begin(pairs, sems):
+        copy.wait()
+
+
 def pack_kernel(
-    parity_ref,
-    state_hbm,
-    adjoint_hbm,
-    neighbors_hbm,
-    same_chip_ref,
-    next_chip_ref,
-    adjoint_ref,
-    neighbors_ref,
-    first_ref,
-    last_ref,
-    sems,
+    parity_ref, state_ends_ref, adjoint_ends_ref, neighbors_ref, same_chip_ref, next_chip_ref
 ):
-    width, elems = adjoint_ref.shape
+    width, elems = adjoint_ends_ref.shape[0], neighbors_ref.shape[1]
     final = elems - LANES
-    copies = begin(
-        [
-            (neighbors_hbm, neighbors_ref),
-            (state_hbm.at[:, :LANES], first_ref),
-            (state_hbm.at[:, final:], last_ref),
-            (adjoint_hbm, adjoint_ref),
-        ],
-        sems,
-    )
     low = lane(width) < HALO
     rows = same_chip_ref.shape[0] - width
-    copies[0].wait()
 
     def codes(first):
         distance, linked, _ = offsets(neighbors_ref[:, first : first + LANES], first, elems)
         code = jnp.where(linked, distance + (HALO + 1), 0).astype(F32)
         return half_roll(padded_rows(code, rows)).astype(BF16)
 
+    def adjoint(first):
+        return half_roll(adjoint_ends_ref[:, first : first + LANES].astype(F32))
+
     up_code, down_code = codes(final), codes(0)
-    for copy in copies[1:]:
-        copy.wait()
-
-    def adjoint(first):
-        return half_roll(adjoint_ref[:, first : first + LANES].astype(F32))
-
-    up = jnp.where(low, adjoint(final), last_ref[...].astype(F32)).astype(BF16)
-    down = jnp.where(low, first_ref[...].astype(F32), adjoint(0)).astype(BF16)
+    up = jnp.where(low, adjoint(LANES), state_ends_ref[:, LANES:].astype(F32)).astype(BF16)
+    down = jnp.where(low, state_ends_ref[:, :LANES].astype(F32), adjoint(0)).astype(BF16)
 
     @pl.when(parity_ref[0] == 0)
     def _():
@@ -166,69 +155,46 @@
         x_ref[start : start + rest, lanes] = one[MAIN:, :]
 
 
-def side_by_side(w_ref, start, tiles_ref, first, count):
-    width = tiles_ref.shape[1]
+def side_by_side(w_ref, tiles_ref):
+    count, width, _ = tiles_ref.shape
     for k in range(count):
-        at = start + k * MAIN
-        w_ref[:, at : at + MAIN] = tiles_ref[first + k, :, :MAIN]
-    w_ref[:, start + count * MAIN : start + count * width] = jnp.concatenate(
-        [tiles_ref[first + k, :, MAIN:] for k in range(count)], axis=1
+        w_ref[:, k * MAIN : (k + 1) * MAIN] = tiles_ref[k, :, :MAIN]
+    w_ref[:, count * MAIN :] = jnp.concatenate(
+        [tiles_ref[k, :, MAIN:] for k in range(count)], axis=1
     )
 
 
 def inner_kernel(
     adjoint_ref,
     neighbors_ref,
-    source_hbm,
-    metric_hbm,
-    basis_hbm,
-    faces_hbm,
-    precond_hbm,
-    traction_tile_hbm,
-    mode_hbm,
-    wall_node_hbm,
-    wall_target_hbm,
-    partial_ref,
-    inner_ref,
-    w_faces_ref,
-    traction_t_ref,
-    srow_ref,
-    out_modes_ref,
-    out_traction_ref,
+    source_ref,
     metric_ref,
-    precond_ref,
-    x_ref,
-    w_ref,
     basis_ref,
     faces_ref,
-    source_ref,
+    precond_ref,
     traction_tile_ref,
     mode_ref,
     wall_node_ref,
     wall_target_ref,
-    sems,
+    partial_ref,
+    inner_ref,
+    w_faces_ref,
+    maps_ref,
+    edge_traction_ref,
+    edge_inverse_ref,
+    edge_hot_ref,
+    srow_ref,
+    out_modes_ref,
+    out_traction_ref,
+    metric_out_ref,
+    precond_out_ref,
+    x_ref,
+    w_ref,
 ):
     width, elems = adjoint_ref.shape
     geo, count = basis_ref.shape[0], faces_ref.shape[0]
     tail = width - MAIN
-    nodes = mode_ref.shape[0]
-    half = geo // 2
-    copies = begin(
-        [
-            (metric_hbm, metric_ref),
-            (wall_node_hbm, wall_node_ref),
-            (wall_target_hbm, wall_target_ref),
-            (mode_hbm, mode_ref),
-            (faces_hbm, faces_ref),
-            (basis_hbm.at[:half], basis_ref.at[:half]),
-            (source_hbm, source_ref),
-            (precond_hbm, precond_ref),
-            (traction_tile_hbm, traction_tile_ref),
-            (basis_hbm.at[half:], basis_ref.at[half:]),
-        ],
-        sems,
-    )
-
+    nodes, lanes = mode_ref.shape
     distance, linked, position = offsets(neighbors_ref[...], 0, elems)
     target = jnp.where(linked, (position + distance).astype(F32), NOWHERE)
     span = LANES + 2 * HALO
@@ -243,28 +209,19 @@
         gathered = mm_nt(adjoint_ref[:, start : start + span], named)
         spread(x_ref, base, count, slice(b * LANES, (b + 1) * LANES), gathered)
 
-    for copy in copies[:4]:
-        copy.wait()
     value = adjoint_ref[...].astype(F32)
     for k in range(geo):
         scaled = (value * metric_ref[k : k + 1, :]).astype(BF16)
-        start = k // half * half * width
-        main = start + k % half * MAIN
-        x_ref[main : main + MAIN, :] = scaled[:MAIN, :]
-        rest = start + half * MAIN + k % half * tail
-        x_ref[rest : rest + tail, :] = scaled[MAIN:, :]
-
-    copies[4].wait()
-    side_by_side(w_faces_ref, 0, faces_ref, 0, count)
+        x_ref[k * MAIN : (k + 1) * MAIN, :] = scaled[:MAIN, :]
+        start = geo * MAIN + k * tail
+        x_ref[start : start + tail, :] = scaled[MAIN:, :]
+    side_by_side(w_faces_ref, faces_ref)
     total = mm(w_faces_ref[...], x_ref[base:, :])
-    middle = half * width
-    copies[5].wait()
-    side_by_side(w_ref, 0, basis_ref, 0, half)
-    total += mm(w_ref[:, :middle], x_ref[:middle, :])
-    for copy in copies[6:]:
-        copy.wait()
-    side_by_side(w_ref, middle, basis_ref, half, half)
-    total += mm(w_ref[:, middle:], x_ref[middle:base, :])
+    side_by_side(w_ref, basis_ref)
+    total += mm(w_ref[...], x_ref[:base, :])
+    metric_out_ref[...] = metric_ref[...]
+    precond_out_ref[...] = precond_ref[...]
+
     node = wall_node_ref[...]
     on_wall = node >= 0
     owner = jnp.where(on_wall, node // nodes, 0).astype(F32)
@@ -284,39 +241,49 @@
     partial_ref[:, :LANES] = rest[:, :LANES]
     partial_ref[:, LANES:] = rest[:, last:]
 
+    traction_t = transposed(traction_tile_ref[...]).astype(BF16)
+    maps_ref[:width, :] = precond_ref[...]
+    both = mm(traction_t, precond_ref[...])
+    coarse = both.astype(BF16)
+    maps_ref[width : width + lanes, :] = coarse
+    maps_ref[width + lanes :, :] = (both - coarse.astype(F32)).astype(BF16)
+    edge_traction_ref[:, :LANES] = mm(traction_t, adjoint_ref[:, :LANES])
+    edge_traction_ref[:, LANES:] = mm(traction_t, adjoint_ref[:, last:])
     update = mm(precond_ref[...], rest[:, LANES:last].astype(BF16))
-    inverse = 1.0 / metric_ref[0:1, LANES:last]
-    inner = (value[:, LANES:last] + update * inverse).astype(BF16)
+    inverse = 1.0 / metric_ref[0:1, :]
+    edge_inverse_ref[...] = jnp.concatenate([inverse[:, :LANES], inverse[:, last:]], axis=1)
+    inner = (value[:, LANES:last] + update * inverse[:, LANES:last]).astype(BF16)
     inner_ref[...] = inner
-    traction_t = transposed(traction_tile_ref[...]).astype(BF16)
-    traction_t_ref[...] = traction_t
     traction = mm(traction_t, inner).astype(BF16)
 
     place = lax.broadcasted_iota(jnp.int32, (slots, last - LANES), 0).astype(F32)
     out_traction_ref[...] = mm_nt(hot(place, elem_slot[:, LANES:last]), traction)
+    edge_slot = jnp.concatenate([elem_slot[:, :LANES], elem_slot[:, last:]], axis=1)
+    edge_hot_ref[...] = hot(place, edge_slot)
 
 
 def edge_kernel(
     parity_ref,
+    next_chip_ref,
     same_chip_ref,
-    next_chip_ref,
-    adjoint_ref,
-    metric_ref,
+    adjoint_ends_ref,
     partial_ref,
     inner_ref,
     w_faces_ref,
-    precond_ref,
-    traction_t_ref,
-    srow_ref,
+    maps_ref,
+    edge_traction_ref,
+    edge_inverse_ref,
+    edge_hot_ref,
     out_modes_ref,
     out_traction_ref,
     new_adjoint_ref,
     send_ref,
     x_ref,
 ):
-    width, elems = adjoint_ref.shape
+    width, elems = new_adjoint_ref.shape
     count = w_faces_ref.shape[1] // width
     last = elems - LANES
+    slots, lanes = out_modes_ref.shape
     message = adjoint_halo(parity_ref[0], same_chip_ref[...], next_chip_ref[...])
     halo, code = message[:width, :].astype(BF16), message[width : width + 8, :]
     position = lane(8)
@@ -334,28 +301,22 @@
         ],
         axis=1,
     )
-    update = mm(precond_ref[...], rest.astype(BF16))
-
-    def ends(x):
-        return jnp.concatenate([x[:, :LANES], x[:, last:]], axis=1)
-
-    inverse = 1.0 / ends(metric_ref[0:1, :])
-    edge = (ends(adjoint_ref[...]).astype(F32) + update * inverse).astype(BF16)
+    update = mm(maps_ref[...], rest.astype(BF16)) * edge_inverse_ref[...]
+    fine = update[width : width + lanes, :] + update[width + lanes :, :]
+    traction = (edge_traction_ref[...] + fine).astype(BF16)
+    out_traction = out_traction_ref[...] + mm_nt(edge_hot_ref[...], traction)
+    both = [x.reshape(slots // CAP, CAP, lanes) for x in (out_modes_ref[...], out_traction)]
+    send_ref[...] = jnp.concatenate(both, axis=1).reshape(2 * slots, lanes).astype(BF16)
+    edge = (adjoint_ends_ref[...].astype(F32) + update[:width, :]).astype(BF16)
     new_adjoint_ref[:, :LANES] = edge[:, :LANES]
     new_adjoint_ref[:, LANES:last] = inner_ref[...]
     new_adjoint_ref[:, last:] = edge[:, LANES:]
-    traction = mm(traction_t_ref[...], edge).astype(BF16)
-    slots, lanes = out_modes_ref.shape
-    place = lax.broadcasted_iota(jnp.int32, (slots, 2 * LANES), 0).astype(F32)
-    out_traction = out_traction_ref[...] + mm_nt(hot(place, ends(srow_ref[0:1, :])), traction)
-    both = [x.reshape(slots // CAP, CAP, lanes) for x in (out_modes_ref[...], out_traction)]
-    send_ref[...] = jnp.concatenate(both, axis=1).reshape(2 * slots, lanes).astype(BF16)
 
 
 def forward_kernel(
     parity_ref,
+    next_chip_ref,
     same_chip_ref,
-    next_chip_ref,
     metric_ref,
     precond_ref,
     neighbors_ref,
@@ -556,15 +517,25 @@
         return (x.shape, x.dtype)
 
     message = ((width + 16, LANES), BF16)
-    same_chip, next_chip, adjoint, neighbors = call(
+    ends = ((width, 2 * LANES), BF16)
+    state_ends, adjoint_ends, neighbors = call(
+        load_kernel,
+        "load",
+        [ends, ends, like(neighbors)],
+        [],
+        (state, adjoint, neighbors),
+        1000,
+        "fff",
+        copies=5,
+    )
+    same_chip, next_chip = call(
         pack_kernel,
         "pack",
-        [message, message, like(adjoint), like(neighbors)],
-        [((width, LANES), BF16), ((width, LANES), BF16)],
-        (parity, state, adjoint, neighbors),
-        1000,
-        "sfff",
-        copies=4,
+        [message, message],
+        [],
+        (parity, state_ends, adjoint_ends, neighbors),
+        10**10,
+        "snnn",
     )
     pairs = [(i, i + 1) for i in range(1, devices - 1, 2)]
     next_chip = lax.ppermute(next_chip, "elem", pairs + [(j, i) for i, j in pairs])
@@ -575,7 +546,10 @@
         partial,
         inner,
         w_faces,
-        traction_t,
+        maps,
+        edge_traction,
+        edge_inverse,
+        edge_hot,
         srow,
         out_modes,
         out_traction,
@@ -588,7 +562,10 @@
             ((width, 2 * LANES), F32),
             ((width, elems - 2 * LANES), BF16),
             ((width, faces * width), BF16),
-            ((lanes, width), BF16),
+            ((width + 2 * lanes, width), BF16),
+            ((lanes, 2 * LANES), F32),
+            ((1, 2 * LANES), F32),
+            ((slots, 2 * LANES), BF16),
             ((8, elems), F32),
             ((slots, lanes), F32),
             ((slots, lanes), F32),
@@ -598,13 +575,6 @@
         [
             (((geo + faces) * width, elems), BF16),
             ((width, geo * width), BF16),
-            like(basis_tiles),
-            like(face_tiles),
-            like(source),
-            like(traction_tile),
-            like(mode_rows),
-            like(wall_node),
-            like(wall_target),
         ],
         (
             adjoint,
@@ -620,8 +590,7 @@
             wall_target,
         ),
         (geo + faces + 3) * unit,
-        "nnfffffffff",
-        copies=10,
+        "nnnnnnnnnnn",
     )
     new_adjoint, send = call(
         edge_kernel,
@@ -630,16 +599,16 @@
         [((faces * width, LANES), BF16)],
         (
             parity,
+            next_chip,
             same_chip,
-            next_chip,
-            adjoint,
-            metric,
+            adjoint_ends,
             partial,
             inner,
             w_faces,
-            precond,
-            traction_t,
-            srow,
+            maps,
+            edge_traction,
+            edge_inverse,
+            edge_hot,
             out_modes,
             out_traction,
         ),
@@ -668,8 +637,8 @@
         ],
         (
             parity,
+            next_chip,
             same_chip,
-            next_chip,
             metric,
             precond,
             neighbors,

time: 38 us -> 38.1 us (level)
  Pallas kernels: 16.3 us -> 15 us
  starting transfers between devices: 15.7 us -> 16.9 us
    ppermute x1, starting transfers between devices: 1.91 us -> 5.2 us  [on_device(): lax.ppermute(next_chip, 'elem', pairs + [(j, i) for i, j in pairs])]
    ppermute x1, starting transfers between devices: 3.33 us -> 0.09 us  [on_device(): lax.ppermute(same_chip, 'elem', pairs + [(j, i) for i, j in pairs])]
    pallas_call x5 -> x6, Pallas kernels: 16.3 us -> 15 us  [call(): pl.pallas_call(kernel, out_shape=[out_space(shape, dtype) for shape, dtyp...]
    all_to_all x1, starting transfers between devices: 10.5 us -> 11.6 us  [on_device(): received = lax.all_to_all(send, 'elem', 0, 0, tiled=True)]
    unnamed x1 -> x21, local copies, waits for them, and re-layouts: 0.73 us -> 0.79 us
  transfers between devices with their start and end apart: 3 -> 3, of which waited for: 1 -> 1; matrix products, arithmetic and copies ran while one was open for 2% -> 2% of each run, Pallas kernels for 30% -> 27%
where the time goes in v4:
time: 38.1 us; the launch traced here: 37.9 us
  starting transfers between devices  16.9 us (44%)
  Pallas kernels  15 us (39%)
  waiting for transfers between devices  4.29 us (11%)
  between operations  0.87 us (2%)
  local copies, waits for them, and re-layouts  0.79 us (2%)
    pallas_call x6, Pallas kernels, call(): pl.pallas_call(kernel, out_shape=[out_space(shape, dtype) for shape, dtyp...  15 us
    all_to_all x1, starting transfers between devices, on_device(): received = lax.all_to_all(send, 'elem', 0, 0, tiled=True)  11.6 us
    ppermute x1, starting transfers between devices, on_device(): lax.ppermute(next_chip, 'elem', pairs + [(j, i) for i, j in pairs])  5.2 us
    all_to_all x1, waiting for transfers between devices, on_device(): received = lax.all_to_all(send, 'elem', 0, 0, tiled=True)  4.28 us
    unnamed x21, local copies, waits for them, and re-layouts  0.79 us
  transfers between devices with their start and end apart: 3, of which 1 were waited for; matrix products, arithmetic and copies ran while one was open for 2% of the time, Pallas kernels for 27%

profile of v4, /device:TPU:1, one launch (start us, length us, event | category | flops | bytes accessed | tf_op | source)
XLA Modules:
  0.0 37.9 jit_solution(3742967795327382215)
XLA Ops:
  0.6 1.1 %load.1 = (bf16[320,256]{1,0:T(8,128)(2,1)S(1)}, bf16[320,256]{1,0:T(8,128)(2,1)S(1)}, s32[6,512]{1,0:T(8,128)S(1)}) custom-call(bf16[320,512]{1,0:T(8,128)(2,1)} %bitcast.21, bf16[320,512]{1,0:T(8,128)(2,1)} %bitcast.15, s32[6,512]{1,0:T(8,128)} %bitcast.23), custom_call_target="tpu_custom_call" | custom-call | flops 1000 | bytes 667648 | tf_op jit(solution)/shard_map/load/pallas_call | solution.py:477
  1.7 0.0 copy-start
  1.7 0.0 copy-start.1
  1.7 0.0 copy-start.2
  1.8 0.0 copy-start.3
  1.8 0.0 copy-start.4
  1.8 0.0 copy-start.5
  1.8 0.0 copy-start.6
  1.8 0.0 copy-start.7
  1.8 0.0 copy-start.8
  1.8 0.0 copy-start.9
  1.8 0.1 pack.1
  2.0 5.2 %collective-permute-start = (bf16[336,128]{1,0:T(8,128)(2,1)S(1)}, bf16[336,128]{1,0:T(8,128)(2,1)S(1)}, u32[]{:S(2)}, u32[]{:S(2)}) collective-permute-start(bf16[336,128]{1,0:T(8,128)(2,1)S(1)} %get-tuple-element.32), channel_id=1, source_target_pairs={{1,2},{3,4},{5,6},{7,8},{9,10},{11,12},{13,14},{15,16},{17,18},{19... | collective-permute-start | bytes 258056 | tf_op jit(solution)/shard_map/ppermute | solution.py:541
  7.2 0.1 collective-permute-start.1
  7.3 0.0 copy-done
  7.3 0.0 copy-done.1
  7.3 0.0 copy-done.2
  7.3 0.0 copy-done.3
  7.3 0.0 copy-done.4
  7.3 0.0 copy-done.5
  7.4 0.0 copy-done.6
  7.4 0.0 copy-done.7
  7.4 0.0 copy-done.8
  7.4 0.0 copy-done.9
  7.4 3.2 %inner.1 = (f32[320,256]{1,0:T(8,128)S(1)}, bf16[320,256]{1,0:T(8,128)(2,1)S(1)}, bf16[320,1920]{1,0:T(8,128)(2,1)S(1)}, bf16[576,320]{1,0:T(8,128)(2,1)S(1)}, f...) custom-call(bf16[320,512]{1,0:T(8,128)(2,1)S(1)} %bitcast.16, ...), custom_call_target="tpu_custom_call" | custom-call | flops 1782579200 | bytes 3906560 | tf_op jit(solution)/shard_map/inner/pallas_call | solution.py:477
  10.6 0.0 collective-permute-done.next_chip_ref
  10.6 0.0 collective-permute-done.1.same_chip_ref
  10.6 2.3 %edge.1 = (bf16[320,512]{1,0:T(8,128)(2,1)S(1)}, bf16[1024,128]{1,0:T(8,128)(2,1)}) custom-call(s32[1]{0:T(128)} %bitcast.6.parity_ref, bf16[336,128]{1,0:T(8,128)(2,1)S(1)} %collective-permute-done.next_chip_ref, bf16[336,128]{1,0:T(8,128)(2,1)S(1)} %collective-permute-done.1.same_chip_ref, bf16[320,256]{1,0:T(8,128)(2,1)S(1)} %get-tuple-element.31.adjoint_ends_ref, ...), custom_call_target="tpu_custom_call" | custom-call | flops 314572800 | bytes 3343364 | tf_op jit(solution)/shard_map/edge/pallas_call | solution.py:477
  13.0 11.6 %all-to-all-start = ((bf16[64,16,128]{2,1,0:T(8,128)(2,1)}), bf16[64,16,128]{2,1,0:T(8,128)(2,1)S(1)}, u32[]{:S(2)}, u32[]{:S(2)}) async-start(bf16[64,16,128]{2,1,0:T(8,128)(2,1)} %bitcast.9), calls=%async_computation | async-start | bytes 524288 | tf_op jit(solution)/shard_map/all_to_all | solution.py:618
  24.6 0.7 %copy.17 = bf16[512,320]{0,1:T(8,128)(2,1)} copy(bf16[512,320]{0,1:T(8,128)(2,1)S(1)} %bitcast.13) | data formatting | bytes 655360
  25.3 7.0 %forward.1 = (f32[320,512]{1,0:T(8,128)S(1)}, bf16[320,128]{1,0:T(8,128)(2,1)S(1)}, bf16[512,512]{1,0:T(8,128)(2,1)S(1)}, bf16[256,512]{1,0:T(8,128)(2,1)S(1)}) custom-call(s32[1]{0:T(128)} %bitcast.6.parity_ref, bf16[336,128]{1,0:T(8,128)(2,1)S(1)} %collective-permute-done.next_chip_ref, bf16[336,128]{1,0:T(8,128)(2,1)S(1)} %collective-permute-done.1.same_chip_ref, ...), custom_call_target="tpu_custom_call" | custom-call | flops 1782579200 | bytes 4355076 | tf_op jit(solution)/shard_map/forward/pallas_call | solution.py:477
  32.3 4.3 %all-to-all-done = bf16[64,16,128]{2,1,0:T(8,128)(2,1)S(1)} async-done(((bf16[64,16,128]{2,1,0:T(8,128)(2,1)}), bf16[64,16,128]{2,1,0:T(8,128)(2,1)S(1)}, u32[]{:S(2)}, u32[]{:S(2)}) %all-to-all-start) | async-done | bytes 262176 | tf_op jit(solution)/shard_map/all_to_all | solution.py:618
  36.6 1.3 %finish.1 = (bf16[320,512]{1,0:T(8,128)(2,1)}, bf16[256,128]{1,0:T(8,128)(2,1)}) custom-call(f32[8,512]{1,0:T(8,128)S(1)} %get-tuple-element.29.metric_ref, f32[320,512]{1,0:T(8,128)S(1)} %get-tuple-element.46.most_ref, bf16[320,128]{1,0:T(8,128)(2,1)S(1)} %get-tuple-element.47.wall_map_ref, bf16[512,512]{1,0:T(8,128)(2,1)S(1)} %get-tuple-element.48.elem_hot_ref, ...), custom_call_target="tpu_custom_call" | custom-call | flops 209715200 | bytes 1802240 | tf_op jit(solution)/shard_map/finish/pallas_call | solution.py:477
Async XLA Ops:
  1.7 5.6 %copy-start = (bf16[512,320]{0,1:T(8,128)(2,1)S(1)}, bf16[512,320]{0,1:T(8,128)(2,1)}, u32[]{:S(2)}) copy-start(bf16[512,320]{0,1:T(8,128)(2,1)} %param.15) | copy-start | bytes 983044
  1.7 5.6 %copy-start.1 = (bf16[8,320,320]{2,1,0:T(8,128)(2,1)S(1)}, bf16[8,320,320]{2,1,0:T(8,128)(2,1)}, u32[]{:S(2)}) copy-start(bf16[8,320,320]{2,1,0:T(8,128)(2,1)} %basis_hbm.1) | copy-start | bytes 4915204
  1.7 5.6 %copy-start.2 = (bf16[6,320,320]{2,1,0:T(8,128)(2,1)S(1)}, bf16[6,320,320]{2,1,0:T(8,128)(2,1)}, u32[]{:S(2)}) copy-start(bf16[6,320,320]{2,1,0:T(8,128)(2,1)} %faces_hbm.1) | copy-start | bytes 3686404
  1.8 5.6 %copy-start.3 = (bf16[512,320]{0,1:T(8,128)(2,1)S(1)}, bf16[512,320]{0,1:T(8,128)(2,1)}, u32[]{:S(2)}) copy-start(bf16[512,320]{0,1:T(8,128)(2,1)} %param.17) | copy-start | bytes 983044
  1.8 5.6 %copy-start.4 = (bf16[320,320]{1,0:T(8,128)(2,1)S(1)}, bf16[320,320]{1,0:T(8,128)(2,1)}, u32[]{:S(2)}) copy-start(bf16[320,320]{1,0:T(8,128)(2,1)} %precond_ref.1) | copy-start | bytes 614404
  1.8 5.6 %copy-start.5 = (bf16[320,128]{1,0:T(8,128)(2,1)S(1)}, bf16[320,128]{1,0:T(8,128)(2,1)}, u32[]{:S(2)}) copy-start(bf16[320,128]{1,0:T(8,128)(2,1)} %traction_tile_ref.1) | copy-start | bytes 245764
  1.8 5.6 %copy-start.6 = (bf16[256,128]{1,0:T(8,128)(2,1)S(1)}, bf16[256,128]{1,0:T(8,128)(2,1)}, u32[]{:S(2)}) copy-start(bf16[256,128]{1,0:T(8,128)(2,1)} %mode_ref.1) | copy-start | bytes 196612
  1.8 5.6 %copy-start.7 = (f32[8,512]{1,0:T(8,128)S(1)}, f32[8,512]{1,0:T(8,128)}, u32[]{:S(2)}) copy-start(f32[8,512]{1,0:T(8,128)} %metric_ref.1) | copy-start | bytes 49156
  1.8 5.6 %copy-start.8 = (s32[512]{0:T(512)S(1)}, s32[512]{0:T(512)}, u32[]{:S(2)}) copy-start(s32[512]{0:T(512)} %param.26) | copy-start | bytes 6148
  1.8 5.6 %copy-start.9 = (s32[256]{0:T(256)S(1)}, s32[256]{0:T(256)}, u32[]{:S(2)}) copy-start(s32[256]{0:T(256)} %param.27) | copy-start | bytes 3076
  2.0 8.6 %collective-permute-start = (bf16[336,128]{1,0:T(8,128)(2,1)S(1)}, bf16[336,128]{1,0:T(8,128)(2,1)S(1)}, u32[]{:S(2)}, u32[]{:S(2)}) collective-permute-start(bf16[336,128]{1,0:T(8,128)(2,1)S(1)} %get-tuple-element.32), channel_id=1, source_target_pairs={{1,2},{3,4},{5,6},{7,8},{9,10},{11,12},{13,14},{15,16},{17,18},{19... | collective-permute-start | bytes 258056 | tf_op jit(solution)/shard_map/ppermute | solution.py:541
  7.2 3.4 %collective-permute-start.1 = (bf16[336,128]{1,0:T(8,128)(2,1)S(1)}, bf16[336,128]{1,0:T(8,128)(2,1)S(1)}, u32[]{:S(2)}, u32[]{:S(2)}) collective-permute-start(bf16[336,128]{1,0:T(8,128)(2,1)S(1)} %get-tuple-element.33), channel_id=1, source_target_pairs={{0,1},{2,3},{4,5},{6,7},{8,9},{10,11},{12,13},{14,15},{16,17},{18,... | collective-permute-start | bytes 258056 | tf_op jit(solution)/shard_map/ppermute | solution.py:543
  13.0 23.6 %all-to-all-start = ((bf16[64,16,128]{2,1,0:T(8,128)(2,1)}), bf16[64,16,128]{2,1,0:T(8,128)(2,1)S(1)}, u32[]{:S(2)}, u32[]{:S(2)}) async-start(bf16[64,16,128]{2,1,0:T(8,128)(2,1)} %bitcast.9), calls=%async_computation | async-start | bytes 524288 | tf_op jit(solution)/shard_map/all_to_all | solution.py:618

commit v5 on v4

--- a/solution.py
+++ b/solution.py
@@ -179,7 +179,7 @@
     partial_ref,
     inner_ref,
     w_faces_ref,
-    maps_ref,
+    traction_map_ref,
     edge_traction_ref,
     edge_inverse_ref,
     edge_hot_ref,
@@ -242,16 +242,21 @@
     partial_ref[:, LANES:] = rest[:, last:]
 
     traction_t = transposed(traction_tile_ref[...]).astype(BF16)
-    maps_ref[:width, :] = precond_ref[...]
+    update = mm(precond_ref[...], rest[:, LANES:last].astype(BF16))
+    inverse = 1.0 / metric_ref[0:1, :]
+    edge_inverse = jnp.concatenate([inverse[:, :LANES], inverse[:, last:]], axis=1)
+    edge_inverse_ref[...] = edge_inverse
+
     both = mm(traction_t, precond_ref[...])
     coarse = both.astype(BF16)
-    maps_ref[width : width + lanes, :] = coarse
-    maps_ref[width + lanes :, :] = (both - coarse.astype(F32)).astype(BF16)
-    edge_traction_ref[:, :LANES] = mm(traction_t, adjoint_ref[:, :LANES])
-    edge_traction_ref[:, LANES:] = mm(traction_t, adjoint_ref[:, last:])
-    update = mm(precond_ref[...], rest[:, LANES:last].astype(BF16))
-    inverse = 1.0 / metric_ref[0:1, :]
-    edge_inverse_ref[...] = jnp.concatenate([inverse[:, :LANES], inverse[:, last:]], axis=1)
+    two_parts = jnp.concatenate([coarse, (both - coarse.astype(F32)).astype(BF16)], axis=0)
+    product = mm(two_parts, w_faces_ref[...])
+    traction_map_ref[...] = (product[:lanes, :] + product[lanes:, :]).astype(BF16)
+    for k, first in enumerate((0, last)):
+        at = slice(k * LANES, (k + 1) * LANES)
+        own = mm(two_parts, rest[:, first : first + LANES].astype(BF16))
+        own = (own[:lanes, :] + own[lanes:, :]) * edge_inverse[:, at]
+        edge_traction_ref[:, at] = mm(traction_t, adjoint_ref[:, first : first + LANES]) + own
     inner = (value[:, LANES:last] + update * inverse[:, LANES:last]).astype(BF16)
     inner_ref[...] = inner
     traction = mm(traction_t, inner).astype(BF16)
@@ -266,23 +271,17 @@
     parity_ref,
     next_chip_ref,
     same_chip_ref,
-    adjoint_ends_ref,
-    partial_ref,
-    inner_ref,
-    w_faces_ref,
-    maps_ref,
+    traction_map_ref,
     edge_traction_ref,
     edge_inverse_ref,
     edge_hot_ref,
     out_modes_ref,
     out_traction_ref,
-    new_adjoint_ref,
+    x_ref,
     send_ref,
-    x_ref,
 ):
-    width, elems = new_adjoint_ref.shape
-    count = w_faces_ref.shape[1] // width
-    last = elems - LANES
+    width = next_chip_ref.shape[0] - 16
+    count = x_ref.shape[0] // width
     slots, lanes = out_modes_ref.shape
     message = adjoint_halo(parity_ref[0], same_chip_ref[...], next_chip_ref[...])
     halo, code = message[:width, :].astype(BF16), message[width : width + 8, :]
@@ -292,22 +291,32 @@
     row = lax.broadcasted_iota(jnp.int32, (LANES, LANES), 0).astype(F32)
     named = jnp.concatenate([hot(row, target[f : f + 1, :]) for f in range(count)], axis=0)
     spread(x_ref, 0, count, slice(0, LANES), mm_nt(halo, named))
-    owed = mm(w_faces_ref[...], x_ref[...])
-    low = lane(width) < HALO
-    rest = jnp.concatenate(
-        [
-            partial_ref[:, :LANES] - jnp.where(low, owed, 0.0),
-            partial_ref[:, LANES:] - jnp.where(low, 0.0, owed),
-        ],
-        axis=1,
-    )
-    update = mm(maps_ref[...], rest.astype(BF16)) * edge_inverse_ref[...]
-    fine = update[width : width + lanes, :] + update[width + lanes :, :]
-    traction = (edge_traction_ref[...] + fine).astype(BF16)
-    out_traction = out_traction_ref[...] + mm_nt(edge_hot_ref[...], traction)
+    owed = mm(traction_map_ref[...], x_ref[...])
+    traction = edge_traction_ref[...] - at_the_ends(owed) * edge_inverse_ref[...]
+    out_traction = out_traction_ref[...] + mm_nt(edge_hot_ref[...], traction.astype(BF16))
     both = [x.reshape(slots // CAP, CAP, lanes) for x in (out_modes_ref[...], out_traction)]
     send_ref[...] = jnp.concatenate(both, axis=1).reshape(2 * slots, lanes).astype(BF16)
-    edge = (adjoint_ends_ref[...].astype(F32) + update[:width, :]).astype(BF16)
+
+
+def at_the_ends(owed):
+    low = lane(owed.shape[0]) < HALO
+    return jnp.concatenate([jnp.where(low, owed, 0.0), jnp.where(low, 0.0, owed)], axis=1)
+
+
+def adjoint_kernel(
+    adjoint_ends_ref,
+    partial_ref,
+    inner_ref,
+    w_faces_ref,
+    precond_ref,
+    edge_inverse_ref,
+    x_ref,
+    new_adjoint_ref,
+):
+    last = new_adjoint_ref.shape[1] - LANES
+    rest = partial_ref[...] - at_the_ends(mm(w_faces_ref[...], x_ref[...]))
+    update = mm(precond_ref[...], rest.astype(BF16)) * edge_inverse_ref[...]
+    edge = (adjoint_ends_ref[...].astype(F32) + update).astype(BF16)
     new_adjoint_ref[:, :LANES] = edge[:, :LANES]
     new_adjoint_ref[:, LANES:last] = inner_ref[...]
     new_adjoint_ref[:, last:] = edge[:, LANES:]
@@ -546,7 +555,7 @@
         partial,
         inner,
         w_faces,
-        maps,
+        traction_map,
         edge_traction,
         edge_inverse,
         edge_hot,
@@ -562,7 +571,7 @@
             ((width, 2 * LANES), F32),
             ((width, elems - 2 * LANES), BF16),
             ((width, faces * width), BF16),
-            ((width + 2 * lanes, width), BF16),
+            ((lanes, faces * width), BF16),
             ((lanes, 2 * LANES), F32),
             ((1, 2 * LANES), F32),
             ((slots, 2 * LANES), BF16),
@@ -592,30 +601,35 @@
         (geo + faces + 3) * unit,
         "nnnnnnnnnnn",
     )
-    new_adjoint, send = call(
+    x, send = call(
         edge_kernel,
         "edge",
-        [((width, elems), BF16), ((2 * slots, lanes), BF16)],
-        [((faces * width, LANES), BF16)],
+        [((faces * width, LANES), BF16), ((2 * slots, lanes), BF16)],
+        [],
         (
             parity,
             next_chip,
             same_chip,
-            adjoint_ends,
-            partial,
-            inner,
-            w_faces,
-            maps,
+            traction_map,
             edge_traction,
             edge_inverse,
             edge_hot,
             out_modes,
             out_traction,
         ),
-        3 * unit,
-        "snnnnnnnnnnnn",
+        unit,
+        "snnnnnnnn",
     )
     received = lax.all_to_all(send, "elem", 0, 0, tiled=True)
+    (new_adjoint,) = call(
+        adjoint_kernel,
+        "adjoint",
+        [((width, elems), BF16)],
+        [],
+        (adjoint_ends, partial, inner, w_faces, precond, edge_inverse, x),
+        2 * unit,
+        "nnnnnnn",
+    )
     most, wall_map, elem_hot, node_hot = call(
         forward_kernel,
         "forward",
@@ -649,7 +663,7 @@
             right_side,
             wall_tile.T,
             wall_target,
-            new_adjoint,
+            x,
         ),
         (geo + faces + 3) * unit,
         "snnnnnnffffffn",

time: 38.1 us -> 37.5 us (0.984)
  waiting for transfers between devices: 4.29 us -> 3.43 us
  Pallas kernels: 15 us -> 15.8 us
  starting transfers between devices: 16.9 us -> 16.3 us
    all_to_all x1, waiting for transfers between devices: 4.28 us -> 3.43 us  [on_device(): received = lax.all_to_all(send, 'elem', 0, 0, tiled=True)]
    pallas_call x6 -> x7, Pallas kernels: 15 us -> 15.8 us  [call(): pl.pallas_call(kernel, out_shape=[out_space(shape, dtype) for shape, dtyp...]
    all_to_all x1, starting transfers between devices: 11.6 us -> 11.1 us  [on_device(): received = lax.all_to_all(send, 'elem', 0, 0, tiled=True)]
  transfers between devices with their start and end apart: 3 -> 3, of which waited for: 1 -> 1; matrix products, arithmetic and copies ran while one was open for 2% -> 2% of each run, Pallas kernels for 27% -> 31%
where the time goes in v5:
time: 37.5 us; the launch traced here: 37.2 us
  starting transfers between devices  16.3 us (43%)
  Pallas kernels  15.8 us (42%)
  waiting for transfers between devices  3.43 us (9%)
  between operations  0.88 us (2%)
  local copies, waits for them, and re-layouts  0.79 us (2%)
    pallas_call x7, Pallas kernels, call(): pl.pallas_call(kernel, out_shape=[out_space(shape, dtype) for shape, dtyp...  15.8 us
    all_to_all x1, starting transfers between devices, on_device(): received = lax.all_to_all(send, 'elem', 0, 0, tiled=True)  11.1 us
    ppermute x1, starting transfers between devices, on_device(): lax.ppermute(next_chip, 'elem', pairs + [(j, i) for i, j in pairs])  5.2 us
    all_to_all x1, waiting for transfers between devices, on_device(): received = lax.all_to_all(send, 'elem', 0, 0, tiled=True)  3.43 us
    unnamed x21, local copies, waits for them, and re-layouts  0.79 us
  transfers between devices with their start and end apart: 3, of which 1 were waited for; matrix products, arithmetic and copies ran while one was open for 2% of the time, Pallas kernels for 31%

profile of v5, /device:TPU:1, one launch (start us, length us, event | category | flops | bytes accessed | tf_op | source)
XLA Modules:
  0.0 37.2 jit_solution(14989905984664055790)
XLA Ops:
  0.6 1.1 %load.1 = (bf16[320,256]{1,0:T(8,128)(2,1)S(1)}, bf16[320,256]{1,0:T(8,128)(2,1)S(1)}, s32[6,512]{1,0:T(8,128)S(1)}) custom-call(bf16[320,512]{1,0:T(8,128)(2,1)} %bitcast.21, bf16[320,512]{1,0:T(8,128)(2,1)} %bitcast.15, s32[6,512]{1,0:T(8,128)} %bitcast.23), custom_call_target="tpu_custom_call" | custom-call | flops 1000 | bytes 667648 | tf_op jit(solution)/shard_map/load/pallas_call | solution.py:486
  1.7 0.0 copy-start
  1.7 0.0 copy-start.1
  1.7 0.0 copy-start.2
  1.8 0.0 copy-start.3
  1.8 0.0 copy-start.4
  1.8 0.0 copy-start.5
  1.8 0.0 copy-start.6
  1.8 0.0 copy-start.7
  1.8 0.0 copy-start.8
  1.8 0.0 copy-start.9
  1.8 0.1 pack.1
  2.0 5.2 %collective-permute-start = (bf16[336,128]{1,0:T(8,128)(2,1)S(1)}, bf16[336,128]{1,0:T(8,128)(2,1)S(1)}, u32[]{:S(2)}, u32[]{:S(2)}) collective-permute-start(bf16[336,128]{1,0:T(8,128)(2,1)S(1)} %get-tuple-element.32), channel_id=1, source_target_pairs={{1,2},{3,4},{5,6},{7,8},{9,10},{11,12},{13,14},{15,16},{17,18},{19... | collective-permute-start | bytes 258056 | tf_op jit(solution)/shard_map/ppermute | solution.py:550
  7.2 0.1 collective-permute-start.1
  7.3 0.0 copy-done
  7.3 0.0 copy-done.1
  7.3 0.0 copy-done.2
  7.3 0.0 copy-done.3
  7.3 0.0 copy-done.4
  7.3 0.0 copy-done.5
  7.4 0.0 copy-done.6
  7.4 0.0 copy-done.7
  7.4 0.0 copy-done.8
  7.4 0.0 copy-done.9
  7.4 3.9 %inner.1 = (f32[320,256]{1,0:T(8,128)S(1)}, bf16[320,256]{1,0:T(8,128)(2,1)S(1)}, bf16[320,1920]{1,0:T(8,128)(2,1)S(1)}, bf16[128,1920]{1,0:T(8,128)(2,1)S(1)}, ...) custom-call(bf16[320,512]{1,0:T(8,128)(2,1)S(1)} %bitcast.16, ...), custom_call_target="tpu_custom_call" | custom-call | flops 1782579200 | bytes 3906560 | tf_op jit(solution)/shard_map/inner/pallas_call | solution.py:486
  11.3 0.0 collective-permute-done.next_chip_ref
  11.3 0.0 collective-permute-done.1.same_chip_ref
  11.3 1.6 %edge.1 = (bf16[1920,128]{1,0:T(8,128)(2,1)S(1)}, bf16[1024,128]{1,0:T(8,128)(2,1)}) custom-call(s32[1]{0:T(128)} %bitcast.6.parity_ref, bf16[336,128]{1,0:T(8,128)(2,1)S(1)} %collective-permute-done.next_chip_ref, bf16[336,128]{1,0:T(8,128)(2,1)S(1)} %collective-permute-done.1.same_chip_ref, bf16[128,1920]{1,0:T(8,128)(2,1)S(1)} %get-tuple-element.36.traction_map_ref, ...), custom_call_target="tpu_custom_call" | custom-call | flops 104857600 | bytes 1582084 | tf_op jit(solution)/shard_map/edge/pallas_call | solution.py:486
  12.9 11.1 %all-to-all-start = ((bf16[64,16,128]{2,1,0:T(8,128)(2,1)}), bf16[64,16,128]{2,1,0:T(8,128)(2,1)S(1)}, u32[]{:S(2)}, u32[]{:S(2)}) async-start(bf16[64,16,128]{2,1,0:T(8,128)(2,1)} %bitcast.9), calls=%async_computation | async-start | bytes 524288 | tf_op jit(solution)/shard_map/all_to_all | solution.py:623
  24.0 0.8 %adjoint.1 = bf16[320,512]{1,0:T(8,128)(2,1)S(1)} custom-call(bf16[320,256]{1,0:T(8,128)(2,1)S(1)} %get-tuple-element.31.adjoint_ends_ref, f32[320,256]{1,0:T(8,128)S(1)} %get-tuple-element.49.partial_ref, bf16[320,256]{1,0:T(8,128)(2,1)S(1)} %get-tuple-element.50.inner_ref, bf16[320,1920]{1,0:T(8,128)(2,1)S(1)} %get-tuple-element.51.w_faces_ref, ...), custom_call_target="tpu_custom_call" | custom-call | flops 209715200 | bytes 2581504 | tf_op jit(solution)/shard_map/adjoint/pallas_call | solution.py:486
  24.8 0.7 %copy.17 = bf16[512,320]{0,1:T(8,128)(2,1)} copy(bf16[512,320]{0,1:T(8,128)(2,1)S(1)} %bitcast.13) | data formatting | bytes 655360
  25.5 7.0 %forward.1 = (f32[320,512]{1,0:T(8,128)S(1)}, bf16[320,128]{1,0:T(8,128)(2,1)S(1)}, bf16[512,512]{1,0:T(8,128)(2,1)S(1)}, bf16[256,512]{1,0:T(8,128)(2,1)S(1)}) custom-call(s32[1]{0:T(128)} %bitcast.6.parity_ref, bf16[336,128]{1,0:T(8,128)(2,1)S(1)} %collective-permute-done.next_chip_ref, bf16[336,128]{1,0:T(8,128)(2,1)S(1)} %collective-permute-done.1.same_chip_ref, ...), custom_call_target="tpu_custom_call" | custom-call | flops 1782579200 | bytes 4518916 | tf_op jit(solution)/shard_map/forward/pallas_call | solution.py:486
  32.5 3.4 %all-to-all-done = bf16[64,16,128]{2,1,0:T(8,128)(2,1)S(1)} async-done(((bf16[64,16,128]{2,1,0:T(8,128)(2,1)}), bf16[64,16,128]{2,1,0:T(8,128)(2,1)S(1)}, u32[]{:S(2)}, u32[]{:S(2)}) %all-to-all-start) | async-done | bytes 262176 | tf_op jit(solution)/shard_map/all_to_all | solution.py:623
  36.0 1.2 %finish.1 = (bf16[320,512]{1,0:T(8,128)(2,1)}, bf16[256,128]{1,0:T(8,128)(2,1)}) custom-call(f32[8,512]{1,0:T(8,128)S(1)} %get-tuple-element.29.metric_ref, f32[320,512]{1,0:T(8,128)S(1)} %get-tuple-element.43.most_ref, bf16[320,128]{1,0:T(8,128)(2,1)S(1)} %get-tuple-element.44.wall_map_ref, bf16[512,512]{1,0:T(8,128)(2,1)S(1)} %get-tuple-element.45.elem_hot_ref, ...), custom_call_target="tpu_custom_call" | custom-call | flops 209715200 | bytes 1802240 | tf_op jit(solution)/shard_map/finish/pallas_call | solution.py:486
Async XLA Ops:
  1.7 5.6 %copy-start = (bf16[512,320]{0,1:T(8,128)(2,1)S(1)}, bf16[512,320]{0,1:T(8,128)(2,1)}, u32[]{:S(2)}) copy-start(bf16[512,320]{0,1:T(8,128)(2,1)} %param.15) | copy-start | bytes 983044
  1.7 5.6 %copy-start.1 = (bf16[8,320,320]{2,1,0:T(8,128)(2,1)S(1)}, bf16[8,320,320]{2,1,0:T(8,128)(2,1)}, u32[]{:S(2)}) copy-start(bf16[8,320,320]{2,1,0:T(8,128)(2,1)} %basis_hbm.1) | copy-start | bytes 4915204
  1.7 5.6 %copy-start.2 = (bf16[6,320,320]{2,1,0:T(8,128)(2,1)S(1)}, bf16[6,320,320]{2,1,0:T(8,128)(2,1)}, u32[]{:S(2)}) copy-start(bf16[6,320,320]{2,1,0:T(8,128)(2,1)} %faces_hbm.1) | copy-start | bytes 3686404
  1.8 5.6 %copy-start.3 = (bf16[512,320]{0,1:T(8,128)(2,1)S(1)}, bf16[512,320]{0,1:T(8,128)(2,1)}, u32[]{:S(2)}) copy-start(bf16[512,320]{0,1:T(8,128)(2,1)} %param.17) | copy-start | bytes 983044
  1.8 5.6 %copy-start.4 = (bf16[320,320]{1,0:T(8,128)(2,1)S(1)}, bf16[320,320]{1,0:T(8,128)(2,1)}, u32[]{:S(2)}) copy-start(bf16[320,320]{1,0:T(8,128)(2,1)} %precond_ref.1) | copy-start | bytes 614404
  1.8 5.6 %copy-start.5 = (bf16[320,128]{1,0:T(8,128)(2,1)S(1)}, bf16[320,128]{1,0:T(8,128)(2,1)}, u32[]{:S(2)}) copy-start(bf16[320,128]{1,0:T(8,128)(2,1)} %traction_tile_ref.1) | copy-start | bytes 245764
  1.8 5.6 %copy-start.6 = (bf16[256,128]{1,0:T(8,128)(2,1)S(1)}, bf16[256,128]{1,0:T(8,128)(2,1)}, u32[]{:S(2)}) copy-start(bf16[256,128]{1,0:T(8,128)(2,1)} %mode_ref.1) | copy-start | bytes 196612
  1.8 5.6 %copy-start.7 = (f32[8,512]{1,0:T(8,128)S(1)}, f32[8,512]{1,0:T(8,128)}, u32[]{:S(2)}) copy-start(f32[8,512]{1,0:T(8,128)} %metric_ref.1) | copy-start | bytes 49156
  1.8 5.6 %copy-start.8 = (s32[512]{0:T(512)S(1)}, s32[512]{0:T(512)}, u32[]{:S(2)}) copy-start(s32[512]{0:T(512)} %param.26) | copy-start | bytes 6148
  1.8 5.6 %copy-start.9 = (s32[256]{0:T(256)S(1)}, s32[256]{0:T(256)}, u32[]{:S(2)}) copy-start(s32[256]{0:T(256)} %param.27) | copy-start | bytes 3076
  2.0 9.3 %collective-permute-start = (bf16[336,128]{1,0:T(8,128)(2,1)S(1)}, bf16[336,128]{1,0:T(8,128)(2,1)S(1)}, u32[]{:S(2)}, u32[]{:S(2)}) collective-permute-start(bf16[336,128]{1,0:T(8,128)(2,1)S(1)} %get-tuple-element.32), channel_id=1, source_target_pairs={{1,2},{3,4},{5,6},{7,8},{9,10},{11,12},{13,14},{15,16},{17,18},{19... | collective-permute-start | bytes 258056 | tf_op jit(solution)/shard_map/ppermute | solution.py:550
  7.2 4.1 %collective-permute-start.1 = (bf16[336,128]{1,0:T(8,128)(2,1)S(1)}, bf16[336,128]{1,0:T(8,128)(2,1)S(1)}, u32[]{:S(2)}, u32[]{:S(2)}) collective-permute-start(bf16[336,128]{1,0:T(8,128)(2,1)S(1)} %get-tuple-element.33), channel_id=1, source_target_pairs={{0,1},{2,3},{4,5},{6,7},{8,9},{10,11},{12,13},{14,15},{16,17},{18,... | collective-permute-start | bytes 258056 | tf_op jit(solution)/shard_map/ppermute | solution.py:552
  12.9 23.1 %all-to-all-start = ((bf16[64,16,128]{2,1,0:T(8,128)(2,1)}), bf16[64,16,128]{2,1,0:T(8,128)(2,1)S(1)}, u32[]{:S(2)}, u32[]{:S(2)}) async-start(bf16[64,16,128]{2,1,0:T(8,128)(2,1)} %bitcast.9), calls=%async_computation | async-start | bytes 524288 | tf_op jit(solution)/shard_map/all_to_all | solution.py:623

commit v6 on v5

--- a/solution.py
+++ b/solution.py
@@ -250,8 +250,7 @@
     both = mm(traction_t, precond_ref[...])
     coarse = both.astype(BF16)
     two_parts = jnp.concatenate([coarse, (both - coarse.astype(F32)).astype(BF16)], axis=0)
-    product = mm(two_parts, w_faces_ref[...])
-    traction_map_ref[...] = (product[:lanes, :] + product[lanes:, :]).astype(BF16)
+    traction_map_ref[...] = mm(coarse, w_faces_ref[...]).astype(BF16)
     for k, first in enumerate((0, last)):
         at = slice(k * LANES, (k + 1) * LANES)
         own = mm(two_parts, rest[:, first : first + LANES].astype(BF16))

time: 37.5 us -> 37.4 us (level)
  Pallas kernels: 15.8 us -> 15.4 us
where the time goes in v6:
time: 37.4 us; the launch traced here: 37.1 us
  starting transfers between devices  16.6 us (44%)
  Pallas kernels  15.4 us (41%)
  waiting for transfers between devices  3.44 us (9%)
  between operations  0.88 us (2%)
  local copies, waits for them, and re-layouts  0.79 us (2%)
    pallas_call x7, Pallas kernels, call(): pl.pallas_call(kernel, out_shape=[out_space(shape, dtype) for shape, dtyp...  15.4 us
    all_to_all x1, starting transfers between devices, on_device(): received = lax.all_to_all(send, 'elem', 0, 0, tiled=True)  11.3 us
    ppermute x1, starting transfers between devices, on_device(): lax.ppermute(next_chip, 'elem', pairs + [(j, i) for i, j in pairs])  5.2 us
    all_to_all x1, waiting for transfers between devices, on_device(): received = lax.all_to_all(send, 'elem', 0, 0, tiled=True)  3.44 us
    unnamed x21, local copies, waits for them, and re-layouts  0.79 us
  transfers between devices with their start and end apart: 3, of which 1 were waited for; matrix products, arithmetic and copies ran while one was open for 2% of the time, Pallas kernels for 31%

profile of v6, /device:TPU:1, one launch (start us, length us, event | category | flops | bytes accessed | tf_op | source)
XLA Modules:
  0.0 37.1 jit_solution(6255328980212114059)
XLA Ops:
  0.6 1.1 %load.1 = (bf16[320,256]{1,0:T(8,128)(2,1)S(1)}, bf16[320,256]{1,0:T(8,128)(2,1)S(1)}, s32[6,512]{1,0:T(8,128)S(1)}) custom-call(bf16[320,512]{1,0:T(8,128)(2,1)} %bitcast.21, bf16[320,512]{1,0:T(8,128)(2,1)} %bitcast.15, s32[6,512]{1,0:T(8,128)} %bitcast.23), custom_call_target="tpu_custom_call" | custom-call | flops 1000 | bytes 667648 | tf_op jit(solution)/shard_map/load/pallas_call | solution.py:485
  1.7 0.0 copy-start
  1.7 0.0 copy-start.1
  1.7 0.0 copy-start.2
  1.8 0.0 copy-start.3
  1.8 0.0 copy-start.4
  1.8 0.0 copy-start.5
  1.8 0.0 copy-start.6
  1.8 0.0 copy-start.7
  1.8 0.0 copy-start.8
  1.8 0.0 copy-start.9
  1.8 0.1 pack.1
  2.0 5.2 %collective-permute-start = (bf16[336,128]{1,0:T(8,128)(2,1)S(1)}, bf16[336,128]{1,0:T(8,128)(2,1)S(1)}, u32[]{:S(2)}, u32[]{:S(2)}) collective-permute-start(bf16[336,128]{1,0:T(8,128)(2,1)S(1)} %get-tuple-element.32), channel_id=1, source_target_pairs={{1,2},{3,4},{5,6},{7,8},{9,10},{11,12},{13,14},{15,16},{17,18},{19... | collective-permute-start | bytes 258056 | tf_op jit(solution)/shard_map/ppermute | solution.py:549
  7.2 0.1 collective-permute-start.1
  7.3 0.0 copy-done
  7.3 0.0 copy-done.1
  7.3 0.0 copy-done.2
  7.3 0.0 copy-done.3
  7.3 0.0 copy-done.4
  7.3 0.0 copy-done.5
  7.4 0.0 copy-done.6
  7.4 0.0 copy-done.7
  7.4 0.0 copy-done.8
  7.4 0.0 copy-done.9
  7.4 3.5 %inner.1 = (f32[320,256]{1,0:T(8,128)S(1)}, bf16[320,256]{1,0:T(8,128)(2,1)S(1)}, bf16[320,1920]{1,0:T(8,128)(2,1)S(1)}, bf16[128,1920]{1,0:T(8,128)(2,1)S(1)}, ...) custom-call(bf16[320,512]{1,0:T(8,128)(2,1)S(1)} %bitcast.16, ...), custom_call_target="tpu_custom_call" | custom-call | flops 1782579200 | bytes 3906560 | tf_op jit(solution)/shard_map/inner/pallas_call | solution.py:485
  10.9 0.0 collective-permute-done.next_chip_ref
  10.9 0.0 collective-permute-done.1.same_chip_ref
  10.9 1.6 %edge.1 = (bf16[1920,128]{1,0:T(8,128)(2,1)S(1)}, bf16[1024,128]{1,0:T(8,128)(2,1)}) custom-call(s32[1]{0:T(128)} %bitcast.6.parity_ref, bf16[336,128]{1,0:T(8,128)(2,1)S(1)} %collective-permute-done.next_chip_ref, bf16[336,128]{1,0:T(8,128)(2,1)S(1)} %collective-permute-done.1.same_chip_ref, bf16[128,1920]{1,0:T(8,128)(2,1)S(1)} %get-tuple-element.36.traction_map_ref, ...), custom_call_target="tpu_custom_call" | custom-call | flops 104857600 | bytes 1582084 | tf_op jit(solution)/shard_map/edge/pallas_call | solution.py:485
  12.6 11.3 %all-to-all-start = ((bf16[64,16,128]{2,1,0:T(8,128)(2,1)}), bf16[64,16,128]{2,1,0:T(8,128)(2,1)S(1)}, u32[]{:S(2)}, u32[]{:S(2)}) async-start(bf16[64,16,128]{2,1,0:T(8,128)(2,1)} %bitcast.9), calls=%async_computation | async-start | bytes 524288 | tf_op jit(solution)/shard_map/all_to_all | solution.py:622
  23.9 0.8 %adjoint.1 = bf16[320,512]{1,0:T(8,128)(2,1)S(1)} custom-call(bf16[320,256]{1,0:T(8,128)(2,1)S(1)} %get-tuple-element.31.adjoint_ends_ref, f32[320,256]{1,0:T(8,128)S(1)} %get-tuple-element.49.partial_ref, bf16[320,256]{1,0:T(8,128)(2,1)S(1)} %get-tuple-element.50.inner_ref, bf16[320,1920]{1,0:T(8,128)(2,1)S(1)} %get-tuple-element.51.w_faces_ref, ...), custom_call_target="tpu_custom_call" | custom-call | flops 209715200 | bytes 2581504 | tf_op jit(solution)/shard_map/adjoint/pallas_call | solution.py:485
  24.7 0.7 %copy.17 = bf16[512,320]{0,1:T(8,128)(2,1)} copy(bf16[512,320]{0,1:T(8,128)(2,1)S(1)} %bitcast.13) | data formatting | bytes 655360
  25.5 7.0 %forward.1 = (f32[320,512]{1,0:T(8,128)S(1)}, bf16[320,128]{1,0:T(8,128)(2,1)S(1)}, bf16[512,512]{1,0:T(8,128)(2,1)S(1)}, bf16[256,512]{1,0:T(8,128)(2,1)S(1)}) custom-call(s32[1]{0:T(128)} %bitcast.6.parity_ref, bf16[336,128]{1,0:T(8,128)(2,1)S(1)} %collective-permute-done.next_chip_ref, bf16[336,128]{1,0:T(8,128)(2,1)S(1)} %collective-permute-done.1.same_chip_ref, ...), custom_call_target="tpu_custom_call" | custom-call | flops 1782579200 | bytes 4518916 | tf_op jit(solution)/shard_map/forward/pallas_call | solution.py:485
  32.5 3.4 %all-to-all-done = bf16[64,16,128]{2,1,0:T(8,128)(2,1)S(1)} async-done(((bf16[64,16,128]{2,1,0:T(8,128)(2,1)}), bf16[64,16,128]{2,1,0:T(8,128)(2,1)S(1)}, u32[]{:S(2)}, u32[]{:S(2)}) %all-to-all-start) | async-done | bytes 262176 | tf_op jit(solution)/shard_map/all_to_all | solution.py:622
  35.9 1.2 %finish.1 = (bf16[320,512]{1,0:T(8,128)(2,1)}, bf16[256,128]{1,0:T(8,128)(2,1)}) custom-call(f32[8,512]{1,0:T(8,128)S(1)} %get-tuple-element.29.metric_ref, f32[320,512]{1,0:T(8,128)S(1)} %get-tuple-element.43.most_ref, bf16[320,128]{1,0:T(8,128)(2,1)S(1)} %get-tuple-element.44.wall_map_ref, bf16[512,512]{1,0:T(8,128)(2,1)S(1)} %get-tuple-element.45.elem_hot_ref, ...), custom_call_target="tpu_custom_call" | custom-call | flops 209715200 | bytes 1802240 | tf_op jit(solution)/shard_map/finish/pallas_call | solution.py:485
Async XLA Ops:
  1.7 5.6 %copy-start = (bf16[512,320]{0,1:T(8,128)(2,1)S(1)}, bf16[512,320]{0,1:T(8,128)(2,1)}, u32[]{:S(2)}) copy-start(bf16[512,320]{0,1:T(8,128)(2,1)} %param.15) | copy-start | bytes 983044
  1.7 5.6 %copy-start.1 = (bf16[8,320,320]{2,1,0:T(8,128)(2,1)S(1)}, bf16[8,320,320]{2,1,0:T(8,128)(2,1)}, u32[]{:S(2)}) copy-start(bf16[8,320,320]{2,1,0:T(8,128)(2,1)} %basis_hbm.1) | copy-start | bytes 4915204
  1.7 5.6 %copy-start.2 = (bf16[6,320,320]{2,1,0:T(8,128)(2,1)S(1)}, bf16[6,320,320]{2,1,0:T(8,128)(2,1)}, u32[]{:S(2)}) copy-start(bf16[6,320,320]{2,1,0:T(8,128)(2,1)} %faces_hbm.1) | copy-start | bytes 3686404
  1.8 5.6 %copy-start.3 = (bf16[512,320]{0,1:T(8,128)(2,1)S(1)}, bf16[512,320]{0,1:T(8,128)(2,1)}, u32[]{:S(2)}) copy-start(bf16[512,320]{0,1:T(8,128)(2,1)} %param.17) | copy-start | bytes 983044
  1.8 5.6 %copy-start.4 = (bf16[320,320]{1,0:T(8,128)(2,1)S(1)}, bf16[320,320]{1,0:T(8,128)(2,1)}, u32[]{:S(2)}) copy-start(bf16[320,320]{1,0:T(8,128)(2,1)} %precond_ref.1) | copy-start | bytes 614404
  1.8 5.6 %copy-start.5 = (bf16[320,128]{1,0:T(8,128)(2,1)S(1)}, bf16[320,128]{1,0:T(8,128)(2,1)}, u32[]{:S(2)}) copy-start(bf16[320,128]{1,0:T(8,128)(2,1)} %traction_tile_ref.1) | copy-start | bytes 245764
  1.8 5.6 %copy-start.6 = (bf16[256,128]{1,0:T(8,128)(2,1)S(1)}, bf16[256,128]{1,0:T(8,128)(2,1)}, u32[]{:S(2)}) copy-start(bf16[256,128]{1,0:T(8,128)(2,1)} %mode_ref.1) | copy-start | bytes 196612
  1.8 5.6 %copy-start.7 = (f32[8,512]{1,0:T(8,128)S(1)}, f32[8,512]{1,0:T(8,128)}, u32[]{:S(2)}) copy-start(f32[8,512]{1,0:T(8,128)} %metric_ref.1) | copy-start | bytes 49156
  1.8 5.6 %copy-start.8 = (s32[512]{0:T(512)S(1)}, s32[512]{0:T(512)}, u32[]{:S(2)}) copy-start(s32[512]{0:T(512)} %param.26) | copy-start | bytes 6148
  1.8 5.6 %copy-start.9 = (s32[256]{0:T(256)S(1)}, s32[256]{0:T(256)}, u32[]{:S(2)}) copy-start(s32[256]{0:T(256)} %param.27) | copy-start | bytes 3076
  2.0 8.9 %collective-permute-start = (bf16[336,128]{1,0:T(8,128)(2,1)S(1)}, bf16[336,128]{1,0:T(8,128)(2,1)S(1)}, u32[]{:S(2)}, u32[]{:S(2)}) collective-permute-start(bf16[336,128]{1,0:T(8,128)(2,1)S(1)} %get-tuple-element.32), channel_id=1, source_target_pairs={{1,2},{3,4},{5,6},{7,8},{9,10},{11,12},{13,14},{15,16},{17,18},{19... | collective-permute-start | bytes 258056 | tf_op jit(solution)/shard_map/ppermute | solution.py:549
  7.2 3.7 %collective-permute-start.1 = (bf16[336,128]{1,0:T(8,128)(2,1)S(1)}, bf16[336,128]{1,0:T(8,128)(2,1)S(1)}, u32[]{:S(2)}, u32[]{:S(2)}) collective-permute-start(bf16[336,128]{1,0:T(8,128)(2,1)S(1)} %get-tuple-element.33), channel_id=1, source_target_pairs={{0,1},{2,3},{4,5},{6,7},{8,9},{10,11},{12,13},{14,15},{16,17},{18,... | collective-permute-start | bytes 258056 | tf_op jit(solution)/shard_map/ppermute | solution.py:551
  12.6 23.3 %all-to-all-start = ((bf16[64,16,128]{2,1,0:T(8,128)(2,1)}), bf16[64,16,128]{2,1,0:T(8,128)(2,1)S(1)}, u32[]{:S(2)}, u32[]{:S(2)}) async-start(bf16[64,16,128]{2,1,0:T(8,128)(2,1)} %bitcast.9), calls=%async_computation | async-start | bytes 524288 | tf_op jit(solution)/shard_map/all_to_all | solution.py:622
